TPU v7x, 32 devices: a whole 2x2x4 slice. The times are simulated.
32 devices in a mesh: seq: 8 (over y, x, core), head: 4 (over z).
Axes of the slice: x: 2, y: 2, z: 4, core: 2. Of those that a mesh axis runs over, the one named last changes fastest.
Arguments:
- queries: bfloat16 [8192, 32, 128], P('seq', 'head'), may hold values from -6 to 6
- keys: bfloat16 [8192, 32, 128], P('seq', 'head'), may hold values from -6 to 6
- values: bfloat16 [8192, 32, 128], P('seq', 'head'), may hold values from -6 to 6
- out_grad: bfloat16 [8192, 32, 128], P('seq', 'head'), may hold values from -6 to 6
- level_codes: int32 [21, 8192], P(None, ('seq', 'head')), may hold values from 1 to 16
Outputs:
- query_grad: bfloat16 [8192, 32, 128], P('seq', 'head')
- key_grad: bfloat16 [8192, 32, 128], P('seq', 'head')
- value_grad: bfloat16 [8192, 32, 128], P('seq', 'head')
Inputs may be any that keep to these rules, and one draw needn't show every extreme that they name: `level_codes`: level codes are whole numbers.
All inputs are finite; a program needn't handle non-finite values.
Results may differ from a plain program's by a relative error of at most 0.0052.
Values sent between devices are 32-bit elements; how exact they have to be, the bound alone decides.
No kernel may reach another device: no remote copies, remote signals or barrier semaphores. Data moves between devices by JAX's collectives and lax.ppermute only.
A program may use at most 128 MiB of HBM per device.

v0:
```python
import functools

import jax
import jax.numpy as jnp
from jax import lax
from jax.experimental import pallas as pl
from jax.experimental.pallas import tpu as pltpu
from jax.sharding import PartitionSpec as P

F32 = jnp.float32
BF16 = jnp.bfloat16
MIB = 1 << 20


def bits_of(size):
    return size.bit_length() - 1


def dot(a, b):
    return jnp.dot(a, b, preferred_element_type=F32)


def dot_nt(a, b):
    return lax.dot_general(a, b, (((1,), (1,)), ((), ())), preferred_element_type=F32)


def scaled(row, x):
    return (row * x.astype(F32)).astype(BF16)


def stack_levels(parts, axis):
    return parts[0] if len(parts) == 1 else jnp.concatenate(parts, axis=axis)


def level_sources(chunks):
    found = []
    for j in range(bits_of(chunks)):
        for first in range(0, chunks, 2 << j):
            found.append(range(first, first + (1 << j)))
    return found


def bit_of_block(b):
    return jnp.bitwise_and(jnp.right_shift(lax.axis_index("seq"), b), 1)


def states_kernel(pieces, *refs):
    inputs = [refs[n * pieces : (n + 1) * pieces] for n in range(4)]
    kh_ref, vh_ref, gh_ref, qt_ref, level_ref, total_ref, chunk_ref = refs[4 * pieces :]
    heads = kh_ref.shape[1]
    size = kh_ref.shape[2] // pieces
    chunks = chunk_ref.shape[0]
    step = pl.program_id(0)
    for n, (k_ref, v_ref, q_ref, g_ref) in enumerate(zip(*inputs)):
        span = slice(n * size, (n + 1) * size)
        kh_ref[0, :, span] = jnp.swapaxes(k_ref[...], 0, 1)
        vh_ref[0, :, span] = jnp.swapaxes(v_ref[...], 0, 1)
        gh_ref[0, :, span] = jnp.swapaxes(g_ref[...], 0, 1)
        queries = jnp.swapaxes(q_ref[...], 0, 1)
        for h in range(heads):
            qt_ref[0, h, :, span] = queries[h].T
    for h in range(heads):
        chunk_ref[step, h] = dot(kh_ref[0, h].T, vh_ref[0, h])

    @pl.when(step == chunks - 1)
    def _():
        for h in range(heads):
            tiles = [chunk_ref[i, h] for i in range(chunks)]
            total_ref[h] = functools.reduce(jnp.add, tiles)
            for n, sources in enumerate(level_sources(chunks)):
                state = functools.reduce(jnp.add, [tiles[i] for i in sources])
                level_ref[n, h] = state.astype(BF16)


def grads_kernel(first_row, lam_ref, qt_ref, g_ref, state_ref, send_ref, keep_ref, whole_ref):
    chunks, heads, tile, width = g_ref.shape
    half = heads // 2
    levels = lam_ref.shape[0] - first_row

    for core in range(2):

        @pl.when(bit_of_block(0) == core)
        def _():
            for h in range(heads):
                weighted = [
                    stack_levels(
                        [
                            scaled(
                                lam_ref[first_row + b : first_row + b + 1, c * tile : (c + 1) * tile],
                                qt_ref[c, h],
                            )
                            for b in range(levels)
                        ],
                        0,
                    )
                    for c in range(chunks)
                ]
                grad = dot(stack_levels(weighted, 1), g_ref[:, h].reshape(chunks * tile, width))
                parts = [grad[b * width : (b + 1) * width] for b in range(levels)]
                state = state_ref[h]
                whole_ref[h] = state if core == 0 else parts[0]
                for b, part in enumerate([state, *parts[1:]]):
                    spot = b * half + h % half
                    if h // half == core:
                        keep_ref[spot] = part
                    else:
                        send_ref[spot] = part


def make_mask(lam_ref, span, mask_ref):
    tile = mask_ref.shape[0]
    part = min(128, tile)
    source = lax.broadcasted_iota(jnp.int32, (part, part), 0)
    target = lax.broadcasted_iota(jnp.int32, (part, part), 1)
    differ = jnp.where(source <= target, jnp.bitwise_xor(source, target), -1)
    for to in range(0, tile, part):
        lanes = slice(span.start + to, span.start + to + part)
        mask = jnp.where(differ >= 0, lam_ref[0:1, lanes], 0.0)
        for power in range(bits_of(part)):
            mask = jnp.where(differ >= 1 << power, lam_ref[power + 1 : power + 2, lanes], mask)
        mask_ref[to : to + part, to : to + part] = mask
        for at in range(0, tile, part):
            if at < to:
                level = bits_of(at ^ to) + 1
                row = lam_ref[level : level + 1, lanes]
                mask_ref[at : at + part, to : to + part] = jnp.broadcast_to(row, (part, part))
            elif at > to:
                mask_ref[at : at + part, to : to + part] = jnp.zeros((part, part), F32)


def diagonal_tile(key, value, query_t, grad, mask):
    weight_q = (mask * dot_nt(value, grad)).astype(BF16)
    weight_v = (mask * dot(key, query_t)).astype(BF16)
    dk = dot_nt(weight_q, query_t).astype(BF16)
    dv = dot(weight_v, grad).astype(BF16)
    return dot(key.T, weight_q), dk, dv


def first_tile_kernel(
    lam_ref, k_ref, v_ref, qt_ref, g_ref, dqt_ref, dq_ref, dk_ref, dv_ref, mask_ref
):
    del dq_ref
    make_mask(lam_ref, slice(0, mask_ref.shape[0]), mask_ref)

    @pl.loop(0, k_ref.shape[1], unroll=4)
    def _(h):
        dqt_ref[h], dk_ref[0, h], dv_ref[0, h] = diagonal_tile(
            k_ref[0, h], v_ref[0, h], qt_ref[0, h], g_ref[0, h], mask_ref[...]
        )


def local_kernel(
    lam_ref, k_ref, v_ref, qt_ref, g_ref, level_ref, found_ref, dqt_ref,
    dq_in, dk_in, dv_in,
    dq_ref, dk_ref, dv_ref, gin_ref, mask_ref, half_ref,
):
    del dq_in, dk_in, dv_in
    chunks, heads, tile, width = k_ref.shape
    tile_bits = bits_of(tile)
    first_row = tile_bits + bits_of(chunks) + 1
    groups = level_sources(chunks)
    off = (1 - bit_of_block(0)).astype(F32)

    @pl.loop(0, heads, unroll=4)
    def _(h):
        found = found_ref[h]
        half_ref[h] = found.astype(BF16)
        for i in range(chunks):
            gin_ref[i, h] = off * found
        row = lam_ref[first_row : first_row + 1, :tile]
        dqt = dqt_ref[h] + row * dot_nt(half_ref[h], g_ref[0, h])
        dq_ref[0, h] = dqt.astype(BF16).T

    for c in range(1, chunks):
        span = slice(c * tile, (c + 1) * tile)
        make_mask(lam_ref, span, mask_ref)

        @pl.loop(0, heads, unroll=4)
        def _(h):
            query_t, grad = qt_ref[c, h], g_ref[c, h]
            dqt, dk_ref[c, h], dv_ref[c, h] = diagonal_tile(
                k_ref[c, h], v_ref[c, h], query_t, grad, mask_ref[...]
            )
            dqt = dqt + lam_ref[first_row : first_row + 1, span] * dot_nt(half_ref[h], grad)
            for j in range(bits_of(chunks)):
                if c >> j & 1:
                    row = lam_ref[tile_bits + 1 + j : tile_bits + 2 + j, span]
                    first = (c >> j ^ 1) << j
                    sources = range(first, first + (1 << j))
                    dqt = dqt + row * dot_nt(level_ref[groups.index(sources), h], grad)
                    part = dot(scaled(row, query_t), grad)
                    for i in sources:
                        gin_ref[i, h] = gin_ref[i, h] + part
            dq_ref[c, h] = dqt.astype(BF16).T


def pair_kernel(levels, keep_ref, found_ref, *out_refs):
    half = out_refs[0].shape[0]
    for b, out_ref in zip(levels, out_refs):
        for on in range(2):

            @pl.when(bit_of_block(b) == on)
            def _():
                for i in range(half):
                    spot = b * on * half + i
                    out_ref[i] = keep_ref[spot] + found_ref[spot]


def sum_kernel(levels, *refs):
    out_ref = refs[-1]
    for n in range(out_ref.shape[0]):
        for i in range(out_ref.shape[1]):
            parts = [ref[i] for b, ref in zip(levels, refs) if b == n + 1]
            out_ref[n, i] = functools.reduce(jnp.add, parts)


def widen(lam_ref, first_row, lanes, wide_ref):
    for b in range(wide_ref.shape[0]):
        row = lam_ref[first_row + b : first_row + b + 1, lanes]
        wide_ref[b] = jnp.broadcast_to(row, wide_ref.shape[:0:-1]).T


def received(sums_ref, i):
    parts = [sums_ref[b, i] for b in range(sums_ref.shape[0])]
    off = [(1 - bit_of_block(b + 1)).astype(F32) for b in range(len(parts))]
    state = functools.reduce(jnp.add, [w * part for w, part in zip(off, parts)])
    return stack_levels([part.astype(BF16) for part in parts], 0), state


def add_to_query(half, wide_ref, grad, dq):
    width = grad.shape[1]
    dq = dq.astype(F32)
    projected = dot_nt(grad, half)
    for b in range(wide_ref.shape[0]):
        dq = dq + wide_ref[b] * projected[:, b * width : (b + 1) * width]
    return dq.astype(BF16)


def add_to_key_value(state, key, value, dk, dv):
    width = key.shape[1]
    state = state.astype(BF16)
    none = jnp.zeros((width, width), BF16)
    right = jnp.concatenate(
        [
            jnp.concatenate([state.T, none], axis=1),
            jnp.concatenate([none, state], axis=1),
        ],
        axis=0,
    )
    product = dot(jnp.concatenate([value, key], axis=1), right)
    dk = dk.astype(F32) + product[:, :width]
    dv = dv.astype(F32) + product[:, width:]
    return dk.astype(BF16), dv.astype(BF16)


def own_half_kernel(
    first_row, lam_ref, k_ref, v_ref, g_ref, gin_ref, sums_ref, dq_in, dk_in, dv_in,
    dq_ref, dk_ref, dv_ref, wide_ref, half_ref, state_ref,
):
    chunks, _, tile, _ = k_ref.shape
    half = half_ref.shape[0]
    start = bit_of_block(0) * half
    for i in range(half):
        half_ref[i], state_ref[i] = received(sums_ref, i)
    for c in range(chunks):
        widen(lam_ref, first_row, slice(c * tile, (c + 1) * tile), wide_ref)
        for i in range(half):
            h = start + i
            dq_ref[c, h] = add_to_query(half_ref[i], wide_ref, g_ref[c, h], dq_in[c, h])
            dk_ref[c, h], dv_ref[c, h] = add_to_key_value(
                gin_ref[c, h] + state_ref[i], k_ref[c, h], v_ref[c, h], dk_in[c, h], dv_in[c, h]
            )


def final_kernel(
    first_row, lam_ref, k_ref, v_ref, g_ref, dq_in, dk_in, dv_in, gin_ref, sums_ref,
    dq_out, dk_out, dv_out, done_ref, wide_ref, half_ref, state_ref, sems,
):
    chunks, heads, tile, _ = k_ref.shape
    half = half_ref.shape[0]
    outs = (dq_out, dk_out, dv_out)

    pieces = sems.shape[2]
    size = tile // pieces

    def ship(n, c):
        return [
            pltpu.make_async_copy(
                done_ref.at[n, c, pl.ds(i * size, size)],
                outs[n].at[pl.ds(c * tile + i * size, size)],
                sems.at[n, c, i],
            )
            for i in range(pieces)
        ]

    for i in range(half):
        half_ref[i], state_ref[i] = received(sums_ref, i)
    for core in range(2):

        @pl.when(bit_of_block(0) == core)
        def _():
            for c in range(chunks):
                widen(lam_ref, first_row, slice(c * tile, (c + 1) * tile), wide_ref)
                queries, keys, values = [], [], []
                for h in range(heads):
                    query, key, value = dq_in[c, h], dk_in[c, h], dv_in[c, h]
                    if h // half != core:
                        i = h % half
                        query = add_to_query(half_ref[i], wide_ref, g_ref[c, h], query)
                        key, value = add_to_key_value(
                            gin_ref[c, h] + state_ref[i], k_ref[c, h], v_ref[c, h], key, value
                        )
                    queries.append(query)
                    keys.append(key)
                    values.append(value)
                for n, parts in enumerate((queries, keys, values)):
                    done_ref[n, c] = jnp.swapaxes(jnp.stack(parts), 0, 1)
                    for copy in ship(n, c):
                        copy.start()

    for c in range(chunks):
        for n in range(3):
            for copy in ship(n, c):
                copy.wait()


def shape(dims, dtype):
    return jax.ShapeDtypeStruct(dims, dtype)


def params(limit):
    return pltpu.CompilerParams(vmem_limit_bytes=limit * MIB)


def cost(flops, size):
    return pl.CostEstimate(flops=int(flops), bytes_accessed=int(size), transcendentals=0)


def on_device(queries, keys, values, out_grad, level_codes):
    count, heads, width = queries.shape
    scale = width ** (-0.5)
    local_bits = bits_of(count)
    blocks = lax.axis_size("seq")
    tree_bits = bits_of(blocks)
    groups = lax.axis_size("head")
    here = lax.axis_index("seq")
    tile = min(256, count)
    chunks = count // tile
    half = heads // 2
    rows = local_bits + 1 + tree_bits

    def permute(x, apart):
        return lax.ppermute(x, "seq", [(i, i ^ apart) for i in range(blocks)])

    def in_hbm(*arrays):
        return [pltpu.with_memory_space_constraint(x, pltpu.HBM) for x in arrays]

    def near(*arrays):
        return [pltpu.with_memory_space_constraint(x, pltpu.VMEM) for x in arrays]

    pieces = 2 if tile % 256 == 0 else 1
    in_vmem = pl.BlockSpec(memory_space=pltpu.VMEM)
    anywhere = pl.BlockSpec(memory_space=pl.ANY)

    def chunk_block(*dims):
        return pl.BlockSpec((1,) + dims, lambda c: (c,) + (0,) * len(dims))

    def whole(*dims):
        return pl.BlockSpec(dims, lambda c: (0,) * len(dims))

    head_block = chunk_block(heads, tile, width)
    natural = pltpu.VMEM((chunks, heads, tile, width), BF16)
    square = (width, width)
    size = count * heads * width
    groups_in = len(level_sources(chunks))
    queries, keys, values, out_grad = in_hbm(queries, keys, values, out_grad)

    kh, vh, gh, qt, level_state, state = pl.pallas_call(
        functools.partial(states_kernel, pieces),
        grid=(chunks,),
        in_specs=[
            pl.BlockSpec((tile // pieces, heads, width), lambda c, n=n: (pieces * c + n, 0, 0))
            for _ in range(4)
            for n in range(pieces)
        ],
        out_specs=[
            *[head_block] * 3, chunk_block(heads, width, tile),
            whole(groups_in, heads, *square), whole(heads, *square),
        ],
        out_shape=[
            *[natural] * 3, pltpu.VMEM((chunks, heads, width, tile), BF16),
            pltpu.VMEM((groups_in, heads, *square), BF16), pltpu.VMEM((heads, *square), F32),
        ],
        scratch_shapes=[pltpu.VMEM((chunks, heads, *square), F32)],
        compiler_params=params(8),
        cost_estimate=cost(2 * size * width, 8 * size),
        name="states",
    )(*[x for x in (keys, values, queries, out_grad) for _ in range(pieces)])

    group = lax.axis_index("head")
    parts = [
        lax.ppermute(level_codes, "head", [(i, (i + r) % groups) for i in range(groups)])
        for r in range(1, groups)
    ]
    parts, state = lax.optimization_barrier((parts, state))
    parts = jnp.stack([level_codes, *parts])
    codes = jnp.concatenate(
        [
            lax.dynamic_index_in_dim(parts, (group - j) % groups, 0, keepdims=False)[:rows]
            for j in range(groups)
        ],
        axis=1,
    )
    order = jnp.arange(rows)
    factor = jnp.exp2(-0.5 * jnp.maximum(order.astype(F32) - 1.0, 0.0)) / 16.0
    on_bit = jnp.bitwise_and(jnp.right_shift(here, jnp.maximum(order - local_bits - 1, 0)), 1)
    factor = jnp.where(order > local_bits, factor * on_bit.astype(F32), factor)
    lam = codes.astype(F32) * (scale * factor)[:, None]

    wide = tree_bits * half
    send, keep, everything = pl.pallas_call(
        functools.partial(grads_kernel, local_bits + 1),
        in_specs=[in_vmem] * 4,
        out_specs=[in_vmem] * 3,
        out_shape=[pltpu.VMEM((n, *square), F32) for n in (wide, wide, heads)],
        compiler_params=params(4),
        cost_estimate=cost(2 * tree_bits * size * width, 2 * size),
        name="level_grads",
    )(lam, *near(qt, gh, state))
    found = permute(send, 1)
    kh, vh, qt, gh, level_state, keep = near(kh, vh, qt, gh, level_state, keep)

    dqt, *parts = pl.pallas_call(
        first_tile_kernel,
        in_specs=[in_vmem] * 5,
        out_specs=[in_vmem] * 4,
        out_shape=[pltpu.VMEM((heads, width, tile), F32)] + [natural] * 3,
        scratch_shapes=[pltpu.VMEM((tile, tile), F32)],
        compiler_params=params(3),
        cost_estimate=cost(14 * size * tile / chunks, 4 * size),
        name="first_tile",
    )(lam, kh, vh, qt, gh)
    hops = [1 << b | m for b in range(1, tree_bits) for m in range(0, 1 << b, 2)]
    hops.sort(key=lambda hop: (hop & hop - 1) == 0)
    messages = pl.pallas_call(
        functools.partial(pair_kernel, [bits_of(hop) for hop in hops]),
        in_specs=[in_vmem] * 2,
        out_specs=[in_vmem] * len(hops),
        out_shape=[pltpu.VMEM((half, *square), F32)] * len(hops),
        compiler_params=params(2),
        cost_estimate=cost(size, size),
        name="pair",
    )(keep, found)
    *messages, parts, everything = lax.optimization_barrier((*messages, parts, everything))
    arrived = [permute(x, hop) for hop, x in zip(hops, messages)]
    first = permute(everything, 1)
    *parts, gin = pl.pallas_call(
        local_kernel,
        in_specs=[in_vmem] * 8 + [anywhere] * 3,
        out_specs=[in_vmem] * 4,
        out_shape=[natural] * 3 + [pltpu.VMEM((chunks, heads, *square), F32)],
        input_output_aliases={8: 0, 9: 1, 10: 2},
        scratch_shapes=[pltpu.VMEM((tile, tile), F32), pltpu.VMEM((heads, *square), BF16)],
        compiler_params=params(3),
        cost_estimate=cost(14 * size * tile, 4 * size),
        name="local",
    )(lam, kh, vh, qt, gh, level_state, first, *near(dqt, *parts))
    arrived, parts = lax.optimization_barrier((arrived, parts))
    sums_shape = (tree_bits - 1, half, *square)
    mine = pl.pallas_call(
        functools.partial(sum_kernel, [bits_of(hop) for hop in hops]),
        in_specs=[in_vmem] * len(hops),
        out_specs=in_vmem,
        out_shape=pltpu.VMEM(sums_shape, F32),
        compiler_params=params(2),
        cost_estimate=cost(size, size),
        name="sums",
    )(*arrived)
    others = permute(mine, 1)

    kept = [
        pltpu.VMEM((tree_bits - 1, tile, width), F32),
        pltpu.VMEM((half, (tree_bits - 1) * width, width), BF16),
        pltpu.VMEM((half, *square), F32),
    ]
    gin, mine = near(gin, mine)
    parts = pl.pallas_call(
        functools.partial(own_half_kernel, local_bits + 2),
        in_specs=[in_vmem] * 9,
        out_specs=[in_vmem] * 3,
        out_shape=[natural] * 3,
        input_output_aliases={6: 0, 7: 1, 8: 2},
        scratch_shapes=kept,
        compiler_params=params(3),
        cost_estimate=cost((tree_bits + 2) * size * width, 8 * size),
        name="own_half",
    )(lam, kh, vh, gh, gin, mine, *near(*parts))
    others, parts = lax.optimization_barrier((others, parts))
    return pl.pallas_call(
        functools.partial(final_kernel, local_bits + 2),
        in_specs=[in_vmem] * 9,
        out_specs=[anywhere] * 3,
        out_shape=[pltpu.HBM((count, heads, width), BF16)] * 3,
        scratch_shapes=[
            pltpu.VMEM((3, chunks, tile, heads, width), BF16), *kept,
            pltpu.SemaphoreType.DMA((3, chunks, pieces)),
        ],
        compiler_params=params(10),
        cost_estimate=cost((tree_bits + 2) * size * width, 16 * size),
        name="final",
    )(lam, kh, vh, gh, *near(*parts), gin, others)


def solution(mesh):
    tokens = P("seq", "head", None)
    return jax.shard_map(
        on_device,
        mesh=mesh,
        in_specs=(tokens, tokens, tokens, tokens, P(None, ("seq", "head"))),
        out_specs=(tokens, tokens, tokens),
        check_vma=False,
    )
```

profile of v0, /device:TPU:0, one launch (start us, length us, event | category | flops | bytes accessed | tf_op | source)
XLA Modules:
  0.0 38.6 jit_solution(12419275623420872008)
XLA Ops:
  0.6 3.1 %collective-permute-start = (s32[21,256]{1,0:T(8,128)}, s32[21,256]{1,0:T(8,128)S(1)}, u32[]{:S(2)}, u32[]{:S(2)}) collective-permute-start(s32[21,256]{1,0:T(8,128)} %param.9), channel_id=1, source_target_pairs={{0,1},{1,2},{2,3},{3,0},{4,5},{5,6},{6,7},{7,4},{8,9},{9,10},{10,1... | collective-permute-start | bytes 64520 | tf_op jit(solution)/shard_map/ppermute | solution.py:402
  3.7 2.1 %collective-permute-start.2 = (s32[21,256]{1,0:T(8,128)}, s32[21,256]{1,0:T(8,128)S(1)}, u32[]{:S(2)}, u32[]{:S(2)}) collective-permute-start(s32[21,256]{1,0:T(8,128)} %param.9), channel_id=1, source_target_pairs={{0,3},{1,0},{2,1},{3,2},{4,7},{5,4},{6,5},{7,6},{8,11},{9,8},{10,9... | collective-permute-start | bytes 64520 | tf_op jit(solution)/shard_map/ppermute | solution.py:402
  5.8 0.9 %collective-permute-start.1 = (s32[21,256]{1,0:T(8,128)}, s32[21,256]{1,0:T(8,128)S(1)}, u32[]{:S(2)}, u32[]{:S(2)}) collective-permute-start(s32[21,256]{1,0:T(8,128)} %param.9), channel_id=1, source_target_pairs={{0,2},{1,3},{2,0},{3,1},{4,6},{5,7},{6,4},{7,5},{8,10},{9,11},{10,... | collective-permute-start | bytes 64520 | tf_op jit(solution)/shard_map/ppermute | solution.py:402
  6.8 0.0 copy-start
  6.8 5.0 %states.1 = (bf16[4,8,256,128]{3,2,1,0:T(8,128)(2,1)S(1)}, bf16[4,8,256,128]{3,2,1,0:T(8,128)(2,1)S(1)}, bf16[4,8,256,128]{3,2,1,0:T(8,128)(2,1)S(1)}, bf16[4,8,...) custom-call(bf16[1024,8,128]{2,1,0:T(8,128)(2,1)} %refs_1_.1, ...), custom_call_target="tpu_custom_call" | custom-call | flops 268435456 | bytes 8388608 | tf_op jit(solution)/shard_map/states/pallas_call | solution.py:378
  11.8 0.0 collective-permute-done
  11.8 0.0 collective-permute-done.2
  11.8 0.0 collective-permute-done.1
  11.8 0.0 copy-done
  11.9 0.1 fusion.lam_ref
  12.0 1.8 %level_grads.1 = (f32[12,128,128]{2,1,0:T(8,128)S(1)}, f32[12,128,128]{2,1,0:T(8,128)S(1)}, f32[8,128,128]{2,1,0:T(8,128)S(1)}) custom-call(f32[14,1024]{1,0:T(8,128)S(1)} %fusion.lam_ref, bf16[4,8,128,256]{3,2,1,0:T(8,128)(2,1)S(1)} %get-tuple-element.54.qt_ref, bf16[4,8,256,128]{3,2,1,0:T(8,128)(2,1)S(1)} %get-tuple-element.53.g_ref, ...), custom_call_target="tpu_custom_call" | custom-call | flops 805306368 | bytes 2097152 | tf_op jit(solution)/shard_map/level_grads/pallas_call | solution.py:421
  13.8 0.1 collective-permute-start.3
  13.9 2.1 %first_tile.1 = (f32[8,128,256]{2,1,0:T(8,128)S(1)}, bf16[4,8,256,128]{3,2,1,0:T(8,128)(2,1)S(1)}, bf16[4,8,256,128]{3,2,1,0:T(8,128)(2,1)S(1)}, bf16[4,8,256,128]{3,2,1,0:T(8,128)(2,1)S(1)}) custom-call(f32[14,1024]{1,0:T(8,128)S(1)} %fusion.lam_ref, bf16[4,8,256,128]{3,2,1,0:T(8,128)(2,1)S(1)} %get-tuple-element.51.k_ref, ...), custom_call_target="tpu_custom_call" | custom-call | flops 939524096 | bytes 4194304 | tf_op jit(solution)/shard_map/first_tile/pallas_call | solution.py:433
  16.0 0.2 collective-permute-done.3.found_ref
  16.2 0.1 pair.1
  16.3 0.4 %collective-permute-start.7 = (f32[8,128,128]{2,1,0:T(8,128)S(1)}, f32[8,128,128]{2,1,0:T(8,128)S(1)}, u32[]{:S(2)}, u32[]{:S(2)}) collective-permute-start(f32[8,128,128]{2,1,0:T(8,128)S(1)} %get-tuple-element.69), channel_id=1, source_target_pairs={{0,4},{4,0},{8,12},{12,8},{16,20},{20,16},{24,28},{28,24},{1,5},{5... | collective-permute-start | bytes 1572872 | tf_op jit(solution)/shard_map/ppermute | solution.py:353
  16.7 2.4 %collective-permute-start.4 = (f32[4,128,128]{2,1,0:T(8,128)S(1)}, f32[4,128,128]{2,1,0:T(8,128)S(1)}, u32[]{:S(2)}, u32[]{:S(2)}) collective-permute-start(f32[4,128,128]{2,1,0:T(8,128)S(1)} %get-tuple-element.65), channel_id=1, source_target_pairs={{0,24},{4,28},{8,16},{12,20},{16,8},{20,12},{24,0},{28,4},{1,25},{... | collective-permute-start | bytes 786440 | tf_op jit(solution)/shard_map/ppermute | solution.py:353
  19.1 0.5 %collective-permute-start.5 = (f32[4,128,128]{2,1,0:T(8,128)S(1)}, f32[4,128,128]{2,1,0:T(8,128)S(1)}, u32[]{:S(2)}, u32[]{:S(2)}) collective-permute-start(f32[4,128,128]{2,1,0:T(8,128)S(1)} %get-tuple-element.66), channel_id=1, source_target_pairs={{0,8},{4,12},{8,0},{12,4},{16,24},{20,28},{24,16},{28,20},{1,9},{5... | collective-permute-start | bytes 786440 | tf_op jit(solution)/shard_map/ppermute | solution.py:353
  19.7 0.5 %collective-permute-start.6 = (f32[4,128,128]{2,1,0:T(8,128)S(1)}, f32[4,128,128]{2,1,0:T(8,128)S(1)}, u32[]{:S(2)}, u32[]{:S(2)}) collective-permute-start(f32[4,128,128]{2,1,0:T(8,128)S(1)} %get-tuple-element.67), channel_id=1, source_target_pairs={{0,16},{4,20},{8,24},{12,28},{16,0},{20,4},{24,8},{28,12},{1,17},{... | collective-permute-start | bytes 786440 | tf_op jit(solution)/shard_map/ppermute | solution.py:353
  20.2 0.0 collective-permute-done.7.found_ref
  20.2 9.0 %local.1 = (bf16[4,8,256,128]{3,2,1,0:T(8,128)(2,1)S(1)}, bf16[4,8,256,128]{3,2,1,0:T(8,128)(2,1)S(1)}, bf16[4,8,256,128]{3,2,1,0:T(8,128)(2,1)S(1)}, f32[4,8,128,128]{3,2,1,0:T(8,128)S(1)}) custom-call(f32[14,1024]{1,0:T(8,128)S(1)} %fusion.lam_ref, ...), custom_call_target="tpu_custom_call", output_to_operand_aliasing={{0}: (8, {}), {1}: (9, {}), {2}: (10, {})} | custom-call | flops 3758096384 | bytes 4194304 | tf_op jit(solution)/shard_map/local/pallas_call | solution.py:457
  29.2 0.0 collective-permute-done.4.refs_0_
  29.2 2.5 %collective-permute-done.5.refs_1_ = f32[4,128,128]{2,1,0:T(8,128)S(1)} collective-permute-done((f32[4,128,128]{2,1,0:T(8,128)S(1)}, f32[4,128,128]{2,1,0:T(8,128)S(1)}, u32[]{:S(2)}, u32[]{:S(2)}) %collective-permute-start.5) | collective-permute-done | bytes 262176 | tf_op jit(solution)/shard_map/ppermute | solution.py:353
  31.7 0.0 collective-permute-done.6.refs_2_
  31.7 0.1 collective-permute-start.8
  31.8 1.3 %own_half.1 = (bf16[4,8,256,128]{3,2,1,0:T(8,128)(2,1)S(1)}, bf16[4,8,256,128]{3,2,1,0:T(8,128)(2,1)S(1)}, bf16[4,8,256,128]{3,2,1,0:T(8,128)(2,1)S(1)}) custom-call(f32[14,1024]{1,0:T(8,128)S(1)} %fusion.lam_ref, bf16[4,8,256,128]{3,2,1,0:T(8,128)(2,1)S(1)} %get-tuple-element.51.k_ref, ...), custom_call_target="tpu_custom_call", output_to_operand_aliasing={{0}: (6, {}), {1}: (7, {}), {2}: (8, {})} | custom-call | flops 671088640 | bytes 8388608 | tf_op jit(solution)/shard_map/own_half/pallas_call | solution.py:487
  33.1 0.5 %collective-permute-done.8.sums_ref = f32[2,4,128,128]{3,2,1,0:T(8,128)S(1)} collective-permute-done((f32[2,4,128,128]{3,2,1,0:T(8,128)S(1)}, f32[2,4,128,128]{3,2,1,0:T(8,128)S(1)}, u32[]{:S(2)}, u32[]{:S(2)}) %collective-permute-start.8) | collective-permute-done | bytes 524320 | tf_op jit(solution)/shard_map/ppermute | solution.py:353
  33.7 4.7 %final.1 = (bf16[1024,8,128]{2,1,0:T(8,128)(2,1)}, bf16[1024,8,128]{2,1,0:T(8,128)(2,1)}, bf16[1024,8,128]{2,1,0:T(8,128)(2,1)}) custom-call(f32[14,1024]{1,0:T(8,128)S(1)} %fusion.lam_ref, bf16[4,8,256,128]{3,2,1,0:T(8,128)(2,1)S(1)} %get-tuple-element.51.k_ref, bf16[4,8,256,128]{3,2,1,0:T(8,128)(2,1)S(1)} %get-tuple-element.52.v_ref, ...), custom_call_target="tpu_custom_call" | custom-call | flops 671088640 | bytes 16777216 | tf_op jit(solution)/shard_map/final/pallas_call | solution.py:499
  (4 shorter events, 0.1 us)
Async XLA Ops:
  0.6 11.2 %collective-permute-start = (s32[21,256]{1,0:T(8,128)}, s32[21,256]{1,0:T(8,128)S(1)}, u32[]{:S(2)}, u32[]{:S(2)}) collective-permute-start(s32[21,256]{1,0:T(8,128)} %param.9), channel_id=1, source_target_pairs={{0,1},{1,2},{2,3},{3,0},{4,5},{5,6},{6,7},{7,4},{8,9},{9,10},{10,1... | collective-permute-start | bytes 64520 | tf_op jit(solution)/shard_map/ppermute | solution.py:402
  3.7 8.1 %collective-permute-start.2 = (s32[21,256]{1,0:T(8,128)}, s32[21,256]{1,0:T(8,128)S(1)}, u32[]{:S(2)}, u32[]{:S(2)}) collective-permute-start(s32[21,256]{1,0:T(8,128)} %param.9), channel_id=1, source_target_pairs={{0,3},{1,0},{2,1},{3,2},{4,7},{5,4},{6,5},{7,6},{8,11},{9,8},{10,9... | collective-permute-start | bytes 64520 | tf_op jit(solution)/shard_map/ppermute | solution.py:402
  5.8 6.0 %collective-permute-start.1 = (s32[21,256]{1,0:T(8,128)}, s32[21,256]{1,0:T(8,128)S(1)}, u32[]{:S(2)}, u32[]{:S(2)}) collective-permute-start(s32[21,256]{1,0:T(8,128)} %param.9), channel_id=1, source_target_pairs={{0,2},{1,3},{2,0},{3,1},{4,6},{5,7},{6,4},{7,5},{8,10},{9,11},{10,... | collective-permute-start | bytes 64520 | tf_op jit(solution)/shard_map/ppermute | solution.py:402
  6.8 5.1 %copy-start = (s32[21,256]{1,0:T(8,128)S(1)}, s32[21,256]{1,0:T(8,128)}, u32[]{:S(2)}) copy-start(s32[21,256]{1,0:T(8,128)} %param.9) | copy-start | bytes 64516
  13.8 2.4 %collective-permute-start.3 = (f32[12,128,128]{2,1,0:T(8,128)S(1)}, f32[12,128,128]{2,1,0:T(8,128)S(1)}, u32[]{:S(2)}, u32[]{:S(2)}) collective-permute-start(f32[12,128,128]{2,1,0:T(8,128)S(1)} %get-tuple-element.57), channel_id=1, source_target_pairs={{0,4},{4,0},{8,12},{12,8},{16,20},{20,16},{24,28},{28,24},{1,5},{5... | collective-permute-start | bytes 2359304 | tf_op jit(solution)/shard_map/ppermute | solution.py:353
  16.3 3.9 %collective-permute-start.7 = (f32[8,128,128]{2,1,0:T(8,128)S(1)}, f32[8,128,128]{2,1,0:T(8,128)S(1)}, u32[]{:S(2)}, u32[]{:S(2)}) collective-permute-start(f32[8,128,128]{2,1,0:T(8,128)S(1)} %get-tuple-element.69), channel_id=1, source_target_pairs={{0,4},{4,0},{8,12},{12,8},{16,20},{20,16},{24,28},{28,24},{1,5},{5... | collective-permute-start | bytes 1572872 | tf_op jit(solution)/shard_map/ppermute | solution.py:353
  16.7 12.5 %collective-permute-start.4 = (f32[4,128,128]{2,1,0:T(8,128)S(1)}, f32[4,128,128]{2,1,0:T(8,128)S(1)}, u32[]{:S(2)}, u32[]{:S(2)}) collective-permute-start(f32[4,128,128]{2,1,0:T(8,128)S(1)} %get-tuple-element.65), channel_id=1, source_target_pairs={{0,24},{4,28},{8,16},{12,20},{16,8},{20,12},{24,0},{28,4},{1,25},{... | collective-permute-start | bytes 786440 | tf_op jit(solution)/shard_map/ppermute | solution.py:353
  19.1 12.6 %collective-permute-start.5 = (f32[4,128,128]{2,1,0:T(8,128)S(1)}, f32[4,128,128]{2,1,0:T(8,128)S(1)}, u32[]{:S(2)}, u32[]{:S(2)}) collective-permute-start(f32[4,128,128]{2,1,0:T(8,128)S(1)} %get-tuple-element.66), channel_id=1, source_target_pairs={{0,8},{4,12},{8,0},{12,4},{16,24},{20,28},{24,16},{28,20},{1,9},{5... | collective-permute-start | bytes 786440 | tf_op jit(solution)/shard_map/ppermute | solution.py:353
  19.7 12.0 %collective-permute-start.6 = (f32[4,128,128]{2,1,0:T(8,128)S(1)}, f32[4,128,128]{2,1,0:T(8,128)S(1)}, u32[]{:S(2)}, u32[]{:S(2)}) collective-permute-start(f32[4,128,128]{2,1,0:T(8,128)S(1)} %get-tuple-element.67), channel_id=1, source_target_pairs={{0,16},{4,20},{8,24},{12,28},{16,0},{20,4},{24,8},{28,12},{1,17},{... | collective-permute-start | bytes 786440 | tf_op jit(solution)/shard_map/ppermute | solution.py:353
  31.7 2.0 %collective-permute-start.8 = (f32[2,4,128,128]{3,2,1,0:T(8,128)S(1)}, f32[2,4,128,128]{3,2,1,0:T(8,128)S(1)}, u32[]{:S(2)}, u32[]{:S(2)}) collective-permute-start(f32[2,4,128,128]{3,2,1,0:T(8,128)S(1)} %sums.1.sums_ref), channel_id=1, source_target_pairs={{0,4},{4,0},{8,12},{12,8},{16,20},{20,16},{24,28},{28,24},{1,5},{5... | collective-permute-start | bytes 1572872 | tf_op jit(solution)/shard_map/ppermute | solution.py:353
where the time goes:
time: 38.8 us; the launch traced here: 38.6 us
  Pallas kernels  24.2 us (62%)
  starting transfers between devices  10.2 us (26%)
  waiting for transfers between devices  3.22 us (8%)
  between operations  0.95 us (2%)
    pallas_call x1, Pallas kernels, on_device(): pl.pallas_call(local_kernel, in_specs=[in_vmem] * 8 + [anywhere] * 3, out...  9 us
    ppermute x3, starting transfers between devices, on_device(): lax.ppermute(level_codes, 'head', [(i, (i + r) % groups) for i in range(g...  6.11 us
    pallas_call x1, Pallas kernels, on_device(): pl.pallas_call(functools.partial(states_kernel, pieces), grid=(chunks,),...  5 us
    pallas_call x1, Pallas kernels, on_device(): pl.pallas_call(functools.partial(final_kernel, local_bits + 2), in_specs=...  4.74 us
    ppermute x6, starting transfers between devices, permute(): return lax.ppermute(x, 'seq', [(i, i ^ apart) for i in range(blocks)])  4.04 us
    ppermute x6, waiting for transfers between devices, permute(): return lax.ppermute(x, 'seq', [(i, i ^ apart) for i in range(blocks)])  3.21 us
    pallas_call x1, Pallas kernels, on_device(): pl.pallas_call(first_tile_kernel, in_specs=[in_vmem] * 5, out_specs=[in_v...  2.09 us
    pallas_call x1, Pallas kernels, on_device(): pl.pallas_call(functools.partial(grads_kernel, local_bits + 1), in_specs=...  1.84 us
  transfers between devices with their start and end apart: 9, of which 3 were waited for; matrix products, arithmetic and copies ran while one was open for 0% of the time, Pallas kernels for 45%

commit v1 on v0

--- a/solution.py
+++ b/solution.py
@@ -72,7 +72,8 @@
                 level_ref[n, h] = state.astype(BF16)
 
 
-def grads_kernel(first_row, lam_ref, qt_ref, g_ref, state_ref, send_ref, keep_ref, whole_ref):
+def grads_kernel(first_row, own, lam_ref, qt_ref, g_ref, state_ref, *refs):
+    sums_ref, whole_ref = refs[-2:]
     chunks, heads, tile, width = g_ref.shape
     half = heads // 2
     levels = lam_ref.shape[0] - first_row
@@ -82,6 +83,8 @@
         @pl.when(bit_of_block(0) == core)
         def _():
             for h in range(heads):
+                if (h // half == core) != own:
+                    continue
                 weighted = [
                     stack_levels(
                         [
@@ -100,11 +103,7 @@
                 state = state_ref[h]
                 whole_ref[h] = state if core == 0 else parts[0]
                 for b, part in enumerate([state, *parts[1:]]):
-                    spot = b * half + h % half
-                    if h // half == core:
-                        keep_ref[spot] = part
-                    else:
-                        send_ref[spot] = part
+                    sums_ref[b * half + h % half] = part
 
 
 def make_mask(lam_ref, span, mask_ref):
@@ -136,25 +135,10 @@
     return dot(key.T, weight_q), dk, dv
 
 
-def first_tile_kernel(
-    lam_ref, k_ref, v_ref, qt_ref, g_ref, dqt_ref, dq_ref, dk_ref, dv_ref, mask_ref
-):
-    del dq_ref
-    make_mask(lam_ref, slice(0, mask_ref.shape[0]), mask_ref)
-
-    @pl.loop(0, k_ref.shape[1], unroll=4)
-    def _(h):
-        dqt_ref[h], dk_ref[0, h], dv_ref[0, h] = diagonal_tile(
-            k_ref[0, h], v_ref[0, h], qt_ref[0, h], g_ref[0, h], mask_ref[...]
-        )
-
-
 def local_kernel(
-    lam_ref, k_ref, v_ref, qt_ref, g_ref, level_ref, found_ref, dqt_ref,
-    dq_in, dk_in, dv_in,
+    lam_ref, k_ref, v_ref, qt_ref, g_ref, level_ref, found_ref,
     dq_ref, dk_ref, dv_ref, gin_ref, mask_ref, half_ref,
 ):
-    del dq_in, dk_in, dv_in
     chunks, heads, tile, width = k_ref.shape
     tile_bits = bits_of(tile)
     first_row = tile_bits + bits_of(chunks) + 1
@@ -167,11 +151,8 @@
         half_ref[h] = found.astype(BF16)
         for i in range(chunks):
             gin_ref[i, h] = off * found
-        row = lam_ref[first_row : first_row + 1, :tile]
-        dqt = dqt_ref[h] + row * dot_nt(half_ref[h], g_ref[0, h])
-        dq_ref[0, h] = dqt.astype(BF16).T
-
-    for c in range(1, chunks):
+
+    for c in range(chunks):
         span = slice(c * tile, (c + 1) * tile)
         make_mask(lam_ref, span, mask_ref)
 
@@ -417,29 +398,25 @@
     factor = jnp.where(order > local_bits, factor * on_bit.astype(F32), factor)
     lam = codes.astype(F32) * (scale * factor)[:, None]
 
-    wide = tree_bits * half
-    send, keep, everything = pl.pallas_call(
-        functools.partial(grads_kernel, local_bits + 1),
-        in_specs=[in_vmem] * 4,
-        out_specs=[in_vmem] * 3,
-        out_shape=[pltpu.VMEM((n, *square), F32) for n in (wide, wide, heads)],
-        compiler_params=params(4),
-        cost_estimate=cost(2 * tree_bits * size * width, 2 * size),
-        name="level_grads",
-    )(lam, *near(qt, gh, state))
+    kh, vh, qt, gh, level_state, state = near(kh, vh, qt, gh, level_state, state)
+
+    def level_grads(own, before):
+        inputs = [lam, qt, gh, state]
+        return pl.pallas_call(
+            functools.partial(grads_kernel, local_bits + 1, own),
+            in_specs=[in_vmem] * len(inputs) + [anywhere] * len(before),
+            out_specs=[in_vmem] * 2,
+            out_shape=[pltpu.VMEM((n, *square), F32) for n in (tree_bits * half, heads)],
+            input_output_aliases={len(inputs): 1} if before else {},
+            compiler_params=params(4),
+            cost_estimate=cost(tree_bits * size * width, size),
+            name="level_grads",
+        )(*inputs, *before)
+
+    send, everything = level_grads(False, [])
     found = permute(send, 1)
-    kh, vh, qt, gh, level_state, keep = near(kh, vh, qt, gh, level_state, keep)
-
-    dqt, *parts = pl.pallas_call(
-        first_tile_kernel,
-        in_specs=[in_vmem] * 5,
-        out_specs=[in_vmem] * 4,
-        out_shape=[pltpu.VMEM((heads, width, tile), F32)] + [natural] * 3,
-        scratch_shapes=[pltpu.VMEM((tile, tile), F32)],
-        compiler_params=params(3),
-        cost_estimate=cost(14 * size * tile / chunks, 4 * size),
-        name="first_tile",
-    )(lam, kh, vh, qt, gh)
+    keep, everything = level_grads(True, near(everything))
+    (keep,) = near(keep)
     hops = [1 << b | m for b in range(1, tree_bits) for m in range(0, 1 << b, 2)]
     hops.sort(key=lambda hop: (hop & hop - 1) == 0)
     messages = pl.pallas_call(
@@ -451,20 +428,19 @@
         cost_estimate=cost(size, size),
         name="pair",
     )(keep, found)
-    *messages, parts, everything = lax.optimization_barrier((*messages, parts, everything))
+    *messages, everything = lax.optimization_barrier((*messages, everything))
     arrived = [permute(x, hop) for hop, x in zip(hops, messages)]
     first = permute(everything, 1)
     *parts, gin = pl.pallas_call(
         local_kernel,
-        in_specs=[in_vmem] * 8 + [anywhere] * 3,
+        in_specs=[in_vmem] * 7,
         out_specs=[in_vmem] * 4,
         out_shape=[natural] * 3 + [pltpu.VMEM((chunks, heads, *square), F32)],
-        input_output_aliases={8: 0, 9: 1, 10: 2},
         scratch_shapes=[pltpu.VMEM((tile, tile), F32), pltpu.VMEM((heads, *square), BF16)],
         compiler_params=params(3),
         cost_estimate=cost(14 * size * tile, 4 * size),
         name="local",
-    )(lam, kh, vh, qt, gh, level_state, first, *near(dqt, *parts))
+    )(lam, kh, vh, qt, gh, level_state, first)
     arrived, parts = lax.optimization_barrier((arrived, parts))
     sums_shape = (tree_bits - 1, half, *square)
     mine = pl.pallas_call(

time: 38.8 us -> 37.9 us (0.977)
  waiting for transfers between devices: 3.22 us -> 2.54 us
    ppermute x6, waiting for transfers between devices: 3.21 us -> 2.54 us  [permute(): return lax.ppermute(x, 'seq', [(i, i ^ apart) for i in range(blocks)])]
  transfers between devices with their start and end apart: 9 -> 9, of which waited for: 3 -> 3; matrix products, arithmetic and copies ran while one was open for 0% -> 0% of each run, Pallas kernels for 45% -> 49%
where the time goes in v1:
time: 37.9 us; the launch traced here: 37.7 us
  Pallas kernels  24.2 us (64%)
  starting transfers between devices  9.96 us (26%)
  waiting for transfers between devices  2.54 us (7%)
  between operations  0.95 us (3%)
    pallas_call x1, Pallas kernels, on_device(): pl.pallas_call(local_kernel, in_specs=[in_vmem] * 7, out_specs=[in_vmem]...  11 us
    ppermute x3, starting transfers between devices, on_device(): lax.ppermute(level_codes, 'head', [(i, (i + r) % groups) for i in range(g...  6.11 us
    pallas_call x1, Pallas kernels, on_device(): pl.pallas_call(functools.partial(states_kernel, pieces), grid=(chunks,),...  5 us
    pallas_call x1, Pallas kernels, on_device(): pl.pallas_call(functools.partial(final_kernel, local_bits + 2), in_specs=...  4.74 us
    ppermute x6, starting transfers between devices, permute(): return lax.ppermute(x, 'seq', [(i, i ^ apart) for i in range(blocks)])  3.85 us
    ppermute x6, waiting for transfers between devices, permute(): return lax.ppermute(x, 'seq', [(i, i ^ apart) for i in range(blocks)])  2.54 us
    pallas_call x2, Pallas kernels, level_grads(): pl.pallas_call(functools.partial(grads_kernel, local_bits + 1, own), in_s...  1.99 us
    pallas_call x1, Pallas kernels, on_device(): pl.pallas_call(functools.partial(own_half_kernel, local_bits + 2), in_spe...  1.34 us
  transfers between devices with their start and end apart: 9, of which 3 were waited for; matrix products, arithmetic and copies ran while one was open for 0% of the time, Pallas kernels for 49%

profile of v1, /device:TPU:0, one launch (start us, length us, event | category | flops | bytes accessed | tf_op | source)
XLA Modules:
  0.0 37.7 jit_solution(3803418882422681304)
XLA Ops:
  0.6 3.1 %collective-permute-start = (s32[21,256]{1,0:T(8,128)}, s32[21,256]{1,0:T(8,128)S(1)}, u32[]{:S(2)}, u32[]{:S(2)}) collective-permute-start(s32[21,256]{1,0:T(8,128)} %param.9), channel_id=1, source_target_pairs={{0,1},{1,2},{2,3},{3,0},{4,5},{5,6},{6,7},{7,4},{8,9},{9,10},{10,1... | collective-permute-start | bytes 64520 | tf_op jit(solution)/shard_map/ppermute | solution.py:383
  3.7 2.1 %collective-permute-start.2 = (s32[21,256]{1,0:T(8,128)}, s32[21,256]{1,0:T(8,128)S(1)}, u32[]{:S(2)}, u32[]{:S(2)}) collective-permute-start(s32[21,256]{1,0:T(8,128)} %param.9), channel_id=1, source_target_pairs={{0,3},{1,0},{2,1},{3,2},{4,7},{5,4},{6,5},{7,6},{8,11},{9,8},{10,9... | collective-permute-start | bytes 64520 | tf_op jit(solution)/shard_map/ppermute | solution.py:383
  5.8 0.9 %collective-permute-start.1 = (s32[21,256]{1,0:T(8,128)}, s32[21,256]{1,0:T(8,128)S(1)}, u32[]{:S(2)}, u32[]{:S(2)}) collective-permute-start(s32[21,256]{1,0:T(8,128)} %param.9), channel_id=1, source_target_pairs={{0,2},{1,3},{2,0},{3,1},{4,6},{5,7},{6,4},{7,5},{8,10},{9,11},{10,... | collective-permute-start | bytes 64520 | tf_op jit(solution)/shard_map/ppermute | solution.py:383
  6.8 0.0 copy-start
  6.8 5.0 %states.1 = (bf16[4,8,256,128]{3,2,1,0:T(8,128)(2,1)S(1)}, bf16[4,8,256,128]{3,2,1,0:T(8,128)(2,1)S(1)}, bf16[4,8,256,128]{3,2,1,0:T(8,128)(2,1)S(1)}, bf16[4,8,...) custom-call(bf16[1024,8,128]{2,1,0:T(8,128)(2,1)} %refs_1_.1, ...), custom_call_target="tpu_custom_call" | custom-call | flops 268435456 | bytes 8388608 | tf_op jit(solution)/shard_map/states/pallas_call | solution.py:359
  11.8 0.0 collective-permute-done
  11.8 0.0 collective-permute-done.2
  11.8 0.0 collective-permute-done.1
  11.8 0.0 copy-done
  11.9 0.1 fusion.lam_ref
  12.0 1.0 %level_grads.2 = (f32[12,128,128]{2,1,0:T(8,128)S(1)}, f32[8,128,128]{2,1,0:T(8,128)S(1)}) custom-call(f32[14,1024]{1,0:T(8,128)S(1)} %fusion.lam_ref, bf16[4,8,128,256]{3,2,1,0:T(8,128)(2,1)S(1)} %get-tuple-element.48.qt_ref, bf16[4,8,256,128]{3,2,1,0:T(8,128)(2,1)S(1)} %get-tuple-element.47.g_ref, f32[8,128,128]{2,1,0:T(8,128)S(1)} %get-tuple-element.49.state_ref), custom_call_target="tpu_custom_call" | custom-call | flops 402653184 | bytes 1048576 | tf_op jit(solution)/shard_map/level_grads/pallas_call | solution.py:405
  13.0 0.1 collective-permute-start.3
  13.0 1.0 %level_grads.3 = (f32[12,128,128]{2,1,0:T(8,128)S(1)}, f32[8,128,128]{2,1,0:T(8,128)S(1)}) custom-call(f32[14,1024]{1,0:T(8,128)S(1)} %fusion.lam_ref, bf16[4,8,128,256]{3,2,1,0:T(8,128)(2,1)S(1)} %get-tuple-element.48.qt_ref, bf16[4,8,256,128]{3,2,1,0:T(8,128)(2,1)S(1)} %get-tuple-element.47.g_ref, ...), custom_call_target="tpu_custom_call", output_to_operand_aliasing={{1}: (4, {})} | custom-call | flops 402653184 | bytes 1048576 | tf_op jit(solution)/shard_map/level_grads/pallas_call | solution.py:405
  14.0 1.3 %collective-permute-done.3.found_ref = f32[12,128,128]{2,1,0:T(8,128)S(1)} collective-permute-done((f32[12,128,128]{2,1,0:T(8,128)S(1)}, f32[12,128,128]{2,1,0:T(8,128)S(1)}, u32[]{:S(2)}, u32[]{:S(2)}) %collective-permute-start.3) | collective-permute-done | bytes 786464 | tf_op jit(solution)/shard_map/ppermute | solution.py:334
  15.3 0.1 pair.1
  15.4 0.2 collective-permute-start.7
  15.6 2.5 %collective-permute-start.4 = (f32[4,128,128]{2,1,0:T(8,128)S(1)}, f32[4,128,128]{2,1,0:T(8,128)S(1)}, u32[]{:S(2)}, u32[]{:S(2)}) collective-permute-start(f32[4,128,128]{2,1,0:T(8,128)S(1)} %get-tuple-element.57), channel_id=1, source_target_pairs={{0,24},{4,28},{8,16},{12,20},{16,8},{20,12},{24,0},{28,4},{1,25},{... | collective-permute-start | bytes 786440 | tf_op jit(solution)/shard_map/ppermute | solution.py:334
  18.1 0.5 %collective-permute-start.5 = (f32[4,128,128]{2,1,0:T(8,128)S(1)}, f32[4,128,128]{2,1,0:T(8,128)S(1)}, u32[]{:S(2)}, u32[]{:S(2)}) collective-permute-start(f32[4,128,128]{2,1,0:T(8,128)S(1)} %get-tuple-element.58), channel_id=1, source_target_pairs={{0,8},{4,12},{8,0},{12,4},{16,24},{20,28},{24,16},{28,20},{1,9},{5... | collective-permute-start | bytes 786440 | tf_op jit(solution)/shard_map/ppermute | solution.py:334
  18.6 0.5 %collective-permute-start.6 = (f32[4,128,128]{2,1,0:T(8,128)S(1)}, f32[4,128,128]{2,1,0:T(8,128)S(1)}, u32[]{:S(2)}, u32[]{:S(2)}) collective-permute-start(f32[4,128,128]{2,1,0:T(8,128)S(1)} %get-tuple-element.59), channel_id=1, source_target_pairs={{0,16},{4,20},{8,24},{12,28},{16,0},{20,4},{24,8},{28,12},{1,17},{... | collective-permute-start | bytes 786440 | tf_op jit(solution)/shard_map/ppermute | solution.py:334
  19.1 0.0 collective-permute-done.7.found_ref
  19.1 11.0 %local.1 = (bf16[4,8,256,128]{3,2,1,0:T(8,128)(2,1)S(1)}, bf16[4,8,256,128]{3,2,1,0:T(8,128)(2,1)S(1)}, bf16[4,8,256,128]{3,2,1,0:T(8,128)(2,1)S(1)}, f32[4,8,128,128]{3,2,1,0:T(8,128)S(1)}) custom-call(f32[14,1024]{1,0:T(8,128)S(1)} %fusion.lam_ref, bf16[4,8,256,128]{3,2,1,0:T(8,128)(2,1)S(1)} %get-tuple-element.45.k_ref, ...), custom_call_target="tpu_custom_call" | custom-call | flops 3758096384 | bytes 4194304 | tf_op jit(solution)/shard_map/local/pallas_call | solution.py:434
  30.1 0.0 collective-permute-done.4.refs_0_
  30.1 0.7 %collective-permute-done.5.refs_1_ = f32[4,128,128]{2,1,0:T(8,128)S(1)} collective-permute-done((f32[4,128,128]{2,1,0:T(8,128)S(1)}, f32[4,128,128]{2,1,0:T(8,128)S(1)}, u32[]{:S(2)}, u32[]{:S(2)}) %collective-permute-start.5) | collective-permute-done | bytes 262176 | tf_op jit(solution)/shard_map/ppermute | solution.py:334
  30.8 0.0 collective-permute-done.6.refs_2_
  30.9 0.1 collective-permute-start.8
  30.9 1.3 %own_half.1 = (bf16[4,8,256,128]{3,2,1,0:T(8,128)(2,1)S(1)}, bf16[4,8,256,128]{3,2,1,0:T(8,128)(2,1)S(1)}, bf16[4,8,256,128]{3,2,1,0:T(8,128)(2,1)S(1)}) custom-call(f32[14,1024]{1,0:T(8,128)S(1)} %fusion.lam_ref, bf16[4,8,256,128]{3,2,1,0:T(8,128)(2,1)S(1)} %get-tuple-element.45.k_ref, ...), custom_call_target="tpu_custom_call", output_to_operand_aliasing={{0}: (6, {}), {1}: (7, {}), {2}: (8, {})} | custom-call | flops 671088640 | bytes 8388608 | tf_op jit(solution)/shard_map/own_half/pallas_call | solution.py:463
  32.3 0.6 %collective-permute-done.8.sums_ref = f32[2,4,128,128]{3,2,1,0:T(8,128)S(1)} collective-permute-done((f32[2,4,128,128]{3,2,1,0:T(8,128)S(1)}, f32[2,4,128,128]{3,2,1,0:T(8,128)S(1)}, u32[]{:S(2)}, u32[]{:S(2)}) %collective-permute-start.8) | collective-permute-done | bytes 524320 | tf_op jit(solution)/shard_map/ppermute | solution.py:334
  32.8 4.7 %final.1 = (bf16[1024,8,128]{2,1,0:T(8,128)(2,1)}, bf16[1024,8,128]{2,1,0:T(8,128)(2,1)}, bf16[1024,8,128]{2,1,0:T(8,128)(2,1)}) custom-call(f32[14,1024]{1,0:T(8,128)S(1)} %fusion.lam_ref, bf16[4,8,256,128]{3,2,1,0:T(8,128)(2,1)S(1)} %get-tuple-element.45.k_ref, bf16[4,8,256,128]{3,2,1,0:T(8,128)(2,1)S(1)} %get-tuple-element.46.v_ref, ...), custom_call_target="tpu_custom_call" | custom-call | flops 671088640 | bytes 16777216 | tf_op jit(solution)/shard_map/final/pallas_call | solution.py:475
  (4 shorter events, 0.1 us)
Async XLA Ops:
  0.6 11.2 %collective-permute-start = (s32[21,256]{1,0:T(8,128)}, s32[21,256]{1,0:T(8,128)S(1)}, u32[]{:S(2)}, u32[]{:S(2)}) collective-permute-start(s32[21,256]{1,0:T(8,128)} %param.9), channel_id=1, source_target_pairs={{0,1},{1,2},{2,3},{3,0},{4,5},{5,6},{6,7},{7,4},{8,9},{9,10},{10,1... | collective-permute-start | bytes 64520 | tf_op jit(solution)/shard_map/ppermute | solution.py:383
  3.7 8.1 %collective-permute-start.2 = (s32[21,256]{1,0:T(8,128)}, s32[21,256]{1,0:T(8,128)S(1)}, u32[]{:S(2)}, u32[]{:S(2)}) collective-permute-start(s32[21,256]{1,0:T(8,128)} %param.9), channel_id=1, source_target_pairs={{0,3},{1,0},{2,1},{3,2},{4,7},{5,4},{6,5},{7,6},{8,11},{9,8},{10,9... | collective-permute-start | bytes 64520 | tf_op jit(solution)/shard_map/ppermute | solution.py:383
  5.8 6.0 %collective-permute-start.1 = (s32[21,256]{1,0:T(8,128)}, s32[21,256]{1,0:T(8,128)S(1)}, u32[]{:S(2)}, u32[]{:S(2)}) collective-permute-start(s32[21,256]{1,0:T(8,128)} %param.9), channel_id=1, source_target_pairs={{0,2},{1,3},{2,0},{3,1},{4,6},{5,7},{6,4},{7,5},{8,10},{9,11},{10,... | collective-permute-start | bytes 64520 | tf_op jit(solution)/shard_map/ppermute | solution.py:383
  6.8 5.1 %copy-start = (s32[21,256]{1,0:T(8,128)S(1)}, s32[21,256]{1,0:T(8,128)}, u32[]{:S(2)}) copy-start(s32[21,256]{1,0:T(8,128)} %param.9) | copy-start | bytes 64516
  13.0 2.4 %collective-permute-start.3 = (f32[12,128,128]{2,1,0:T(8,128)S(1)}, f32[12,128,128]{2,1,0:T(8,128)S(1)}, u32[]{:S(2)}, u32[]{:S(2)}) collective-permute-start(f32[12,128,128]{2,1,0:T(8,128)S(1)} %get-tuple-element.52), channel_id=1, source_target_pairs={{0,4},{4,0},{8,12},{12,8},{16,20},{20,16},{24,28},{28,24},{1,5},{5... | collective-permute-start | bytes 2359304 | tf_op jit(solution)/shard_map/ppermute | solution.py:334
  15.4 3.7 %collective-permute-start.7 = (f32[8,128,128]{2,1,0:T(8,128)S(1)}, f32[8,128,128]{2,1,0:T(8,128)S(1)}, u32[]{:S(2)}, u32[]{:S(2)}) collective-permute-start(f32[8,128,128]{2,1,0:T(8,128)S(1)} %get-tuple-element.61), channel_id=1, source_target_pairs={{0,4},{4,0},{8,12},{12,8},{16,20},{20,16},{24,28},{28,24},{1,5},{5... | collective-permute-start | bytes 1572872 | tf_op jit(solution)/shard_map/ppermute | solution.py:334
  15.6 14.5 %collective-permute-start.4 = (f32[4,128,128]{2,1,0:T(8,128)S(1)}, f32[4,128,128]{2,1,0:T(8,128)S(1)}, u32[]{:S(2)}, u32[]{:S(2)}) collective-permute-start(f32[4,128,128]{2,1,0:T(8,128)S(1)} %get-tuple-element.57), channel_id=1, source_target_pairs={{0,24},{4,28},{8,16},{12,20},{16,8},{20,12},{24,0},{28,4},{1,25},{... | collective-permute-start | bytes 786440 | tf_op jit(solution)/shard_map/ppermute | solution.py:334
  18.1 12.7 %collective-permute-start.5 = (f32[4,128,128]{2,1,0:T(8,128)S(1)}, f32[4,128,128]{2,1,0:T(8,128)S(1)}, u32[]{:S(2)}, u32[]{:S(2)}) collective-permute-start(f32[4,128,128]{2,1,0:T(8,128)S(1)} %get-tuple-element.58), channel_id=1, source_target_pairs={{0,8},{4,12},{8,0},{12,4},{16,24},{20,28},{24,16},{28,20},{1,9},{5... | collective-permute-start | bytes 786440 | tf_op jit(solution)/shard_map/ppermute | solution.py:334
  18.6 12.2 %collective-permute-start.6 = (f32[4,128,128]{2,1,0:T(8,128)S(1)}, f32[4,128,128]{2,1,0:T(8,128)S(1)}, u32[]{:S(2)}, u32[]{:S(2)}) collective-permute-start(f32[4,128,128]{2,1,0:T(8,128)S(1)} %get-tuple-element.59), channel_id=1, source_target_pairs={{0,16},{4,20},{8,24},{12,28},{16,0},{20,4},{24,8},{28,12},{1,17},{... | collective-permute-start | bytes 786440 | tf_op jit(solution)/shard_map/ppermute | solution.py:334
  30.9 2.0 %collective-permute-start.8 = (f32[2,4,128,128]{3,2,1,0:T(8,128)S(1)}, f32[2,4,128,128]{3,2,1,0:T(8,128)S(1)}, u32[]{:S(2)}, u32[]{:S(2)}) collective-permute-start(f32[2,4,128,128]{3,2,1,0:T(8,128)S(1)} %sums.1.sums_ref), channel_id=1, source_target_pairs={{0,4},{4,0},{8,12},{12,8},{16,20},{20,16},{24,28},{28,24},{1,5},{5... | collective-permute-start | bytes 1572872 | tf_op jit(solution)/shard_map/ppermute | solution.py:334

commit v2 on v1

--- a/solution.py
+++ b/solution.py
@@ -282,22 +282,30 @@
         def _():
             for c in range(chunks):
                 widen(lam_ref, first_row, slice(c * tile, (c + 1) * tile), wide_ref)
-                queries, keys, values = [], [], []
-                for h in range(heads):
-                    query, key, value = dq_in[c, h], dk_in[c, h], dv_in[c, h]
-                    if h // half != core:
-                        i = h % half
-                        query = add_to_query(half_ref[i], wide_ref, g_ref[c, h], query)
-                        key, value = add_to_key_value(
-                            gin_ref[c, h] + state_ref[i], k_ref[c, h], v_ref[c, h], key, value
-                        )
-                    queries.append(query)
-                    keys.append(key)
-                    values.append(value)
-                for n, parts in enumerate((queries, keys, values)):
+
+                def send_out(n, parts):
                     done_ref[n, c] = jnp.swapaxes(jnp.stack(parts), 0, 1)
                     for copy in ship(n, c):
                         copy.start()
+
+                queries, keys, values = [], [], []
+                for h in range(heads):
+                    query = dq_in[c, h]
+                    if h // half != core:
+                        query = add_to_query(half_ref[h % half], wide_ref, g_ref[c, h], query)
+                    queries.append(query)
+                send_out(0, queries)
+                for h in range(heads):
+                    key, value = dk_in[c, h], dv_in[c, h]
+                    if h // half != core:
+                        key, value = add_to_key_value(
+                            gin_ref[c, h] + state_ref[h % half],
+                            k_ref[c, h], v_ref[c, h], key, value,
+                        )
+                    keys.append(key)
+                    values.append(value)
+                send_out(1, keys)
+                send_out(2, values)
 
     for c in range(chunks):
         for n in range(3):
@@ -418,7 +426,7 @@
     keep, everything = level_grads(True, near(everything))
     (keep,) = near(keep)
     hops = [1 << b | m for b in range(1, tree_bits) for m in range(0, 1 << b, 2)]
-    hops.sort(key=lambda hop: (hop & hop - 1) == 0)
+    hops.sort(key=lambda hop: (bits_of(hop), -hop))
     messages = pl.pallas_call(
         functools.partial(pair_kernel, [bits_of(hop) for hop in hops]),
         in_specs=[in_vmem] * 2,

time: 37.9 us -> 39.3 us (1.037)
  waiting for transfers between devices: 2.54 us -> 3.97 us
    ppermute x6, waiting for transfers between devices: 2.54 us -> 3.96 us  [permute(): return lax.ppermute(x, 'seq', [(i, i ^ apart) for i in range(blocks)])]
  transfers between devices with their start and end apart: 9 -> 9, of which waited for: 3 -> 4; matrix products, arithmetic and copies ran while one was open for 0% -> 0% of each run, Pallas kernels for 49% -> 47%
where the time goes in v2:
time: 39.3 us; the launch traced here: 39.1 us
  Pallas kernels  24.1 us (61%)
  starting transfers between devices  9.96 us (25%)
  waiting for transfers between devices  3.97 us (10%)
  between operations  0.95 us (2%)
    pallas_call x1, Pallas kernels, on_device(): pl.pallas_call(local_kernel, in_specs=[in_vmem] * 7, out_specs=[in_vmem]...  11 us
    ppermute x3, starting transfers between devices, on_device(): lax.ppermute(level_codes, 'head', [(i, (i + r) % groups) for i in range(g...  6.11 us
    pallas_call x1, Pallas kernels, on_device(): pl.pallas_call(functools.partial(states_kernel, pieces), grid=(chunks,),...  5 us
    pallas_call x1, Pallas kernels, on_device(): pl.pallas_call(functools.partial(final_kernel, local_bits + 2), in_specs=...  4.7 us
    ppermute x6, waiting for transfers between devices, permute(): return lax.ppermute(x, 'seq', [(i, i ^ apart) for i in range(blocks)])  3.96 us
    ppermute x6, starting transfers between devices, permute(): return lax.ppermute(x, 'seq', [(i, i ^ apart) for i in range(blocks)])  3.85 us
    pallas_call x2, Pallas kernels, level_grads(): pl.pallas_call(functools.partial(grads_kernel, local_bits + 1, own), in_s...  1.99 us
    pallas_call x1, Pallas kernels, on_device(): pl.pallas_call(functools.partial(own_half_kernel, local_bits + 2), in_spe...  1.34 us
  transfers between devices with their start and end apart: 9, of which 4 were waited for; matrix products, arithmetic and copies ran while one was open for 0% of the time, Pallas kernels for 47%

profile of v2, /device:TPU:0, one launch (start us, length us, event | category | flops | bytes accessed | tf_op | source)
XLA Modules:
  0.0 39.1 jit_solution(14614352926957897146)
XLA Ops:
  0.6 3.1 %collective-permute-start = (s32[21,256]{1,0:T(8,128)}, s32[21,256]{1,0:T(8,128)S(1)}, u32[]{:S(2)}, u32[]{:S(2)}) collective-permute-start(s32[21,256]{1,0:T(8,128)} %param.9), channel_id=1, source_target_pairs={{0,1},{1,2},{2,3},{3,0},{4,5},{5,6},{6,7},{7,4},{8,9},{9,10},{10,1... | collective-permute-start | bytes 64520 | tf_op jit(solution)/shard_map/ppermute | solution.py:391
  3.7 2.1 %collective-permute-start.2 = (s32[21,256]{1,0:T(8,128)}, s32[21,256]{1,0:T(8,128)S(1)}, u32[]{:S(2)}, u32[]{:S(2)}) collective-permute-start(s32[21,256]{1,0:T(8,128)} %param.9), channel_id=1, source_target_pairs={{0,3},{1,0},{2,1},{3,2},{4,7},{5,4},{6,5},{7,6},{8,11},{9,8},{10,9... | collective-permute-start | bytes 64520 | tf_op jit(solution)/shard_map/ppermute | solution.py:391
  5.8 0.9 %collective-permute-start.1 = (s32[21,256]{1,0:T(8,128)}, s32[21,256]{1,0:T(8,128)S(1)}, u32[]{:S(2)}, u32[]{:S(2)}) collective-permute-start(s32[21,256]{1,0:T(8,128)} %param.9), channel_id=1, source_target_pairs={{0,2},{1,3},{2,0},{3,1},{4,6},{5,7},{6,4},{7,5},{8,10},{9,11},{10,... | collective-permute-start | bytes 64520 | tf_op jit(solution)/shard_map/ppermute | solution.py:391
  6.8 0.0 copy-start
  6.8 5.0 %states.1 = (bf16[4,8,256,128]{3,2,1,0:T(8,128)(2,1)S(1)}, bf16[4,8,256,128]{3,2,1,0:T(8,128)(2,1)S(1)}, bf16[4,8,256,128]{3,2,1,0:T(8,128)(2,1)S(1)}, bf16[4,8,...) custom-call(bf16[1024,8,128]{2,1,0:T(8,128)(2,1)} %refs_1_.1, ...), custom_call_target="tpu_custom_call" | custom-call | flops 268435456 | bytes 8388608 | tf_op jit(solution)/shard_map/states/pallas_call | solution.py:367
  11.8 0.0 collective-permute-done
  11.8 0.0 collective-permute-done.2
  11.8 0.0 collective-permute-done.1
  11.8 0.0 copy-done
  11.9 0.1 fusion.lam_ref
  12.0 1.0 %level_grads.2 = (f32[12,128,128]{2,1,0:T(8,128)S(1)}, f32[8,128,128]{2,1,0:T(8,128)S(1)}) custom-call(f32[14,1024]{1,0:T(8,128)S(1)} %fusion.lam_ref, bf16[4,8,128,256]{3,2,1,0:T(8,128)(2,1)S(1)} %get-tuple-element.48.qt_ref, bf16[4,8,256,128]{3,2,1,0:T(8,128)(2,1)S(1)} %get-tuple-element.47.g_ref, f32[8,128,128]{2,1,0:T(8,128)S(1)} %get-tuple-element.49.state_ref), custom_call_target="tpu_custom_call" | custom-call | flops 402653184 | bytes 1048576 | tf_op jit(solution)/shard_map/level_grads/pallas_call | solution.py:413
  13.0 0.1 collective-permute-start.3
  13.0 1.0 %level_grads.3 = (f32[12,128,128]{2,1,0:T(8,128)S(1)}, f32[8,128,128]{2,1,0:T(8,128)S(1)}) custom-call(f32[14,1024]{1,0:T(8,128)S(1)} %fusion.lam_ref, bf16[4,8,128,256]{3,2,1,0:T(8,128)(2,1)S(1)} %get-tuple-element.48.qt_ref, bf16[4,8,256,128]{3,2,1,0:T(8,128)(2,1)S(1)} %get-tuple-element.47.g_ref, ...), custom_call_target="tpu_custom_call", output_to_operand_aliasing={{1}: (4, {})} | custom-call | flops 402653184 | bytes 1048576 | tf_op jit(solution)/shard_map/level_grads/pallas_call | solution.py:413
  14.0 1.3 %collective-permute-done.3.found_ref = f32[12,128,128]{2,1,0:T(8,128)S(1)} collective-permute-done((f32[12,128,128]{2,1,0:T(8,128)S(1)}, f32[12,128,128]{2,1,0:T(8,128)S(1)}, u32[]{:S(2)}, u32[]{:S(2)}) %collective-permute-start.3) | collective-permute-done | bytes 786464 | tf_op jit(solution)/shard_map/ppermute | solution.py:342
  15.3 0.1 pair.1
  15.4 0.2 collective-permute-start.7
  15.6 1.5 %collective-permute-start.4 = (f32[4,128,128]{2,1,0:T(8,128)S(1)}, f32[4,128,128]{2,1,0:T(8,128)S(1)}, u32[]{:S(2)}, u32[]{:S(2)}) collective-permute-start(f32[4,128,128]{2,1,0:T(8,128)S(1)} %get-tuple-element.57), channel_id=1, source_target_pairs={{0,8},{4,12},{8,0},{12,4},{16,24},{20,28},{24,16},{28,20},{1,9},{5... | collective-permute-start | bytes 786440 | tf_op jit(solution)/shard_map/ppermute | solution.py:342
  17.1 1.5 %collective-permute-start.5 = (f32[4,128,128]{2,1,0:T(8,128)S(1)}, f32[4,128,128]{2,1,0:T(8,128)S(1)}, u32[]{:S(2)}, u32[]{:S(2)}) collective-permute-start(f32[4,128,128]{2,1,0:T(8,128)S(1)} %get-tuple-element.58), channel_id=1, source_target_pairs={{0,24},{4,28},{8,16},{12,20},{16,8},{20,12},{24,0},{28,4},{1,25},{... | collective-permute-start | bytes 786440 | tf_op jit(solution)/shard_map/ppermute | solution.py:342
  18.6 0.5 %collective-permute-start.6 = (f32[4,128,128]{2,1,0:T(8,128)S(1)}, f32[4,128,128]{2,1,0:T(8,128)S(1)}, u32[]{:S(2)}, u32[]{:S(2)}) collective-permute-start(f32[4,128,128]{2,1,0:T(8,128)S(1)} %get-tuple-element.59), channel_id=1, source_target_pairs={{0,16},{4,20},{8,24},{12,28},{16,0},{20,4},{24,8},{28,12},{1,17},{... | collective-permute-start | bytes 786440 | tf_op jit(solution)/shard_map/ppermute | solution.py:342
  19.1 0.0 collective-permute-done.7.found_ref
  19.1 11.0 %local.1 = (bf16[4,8,256,128]{3,2,1,0:T(8,128)(2,1)S(1)}, bf16[4,8,256,128]{3,2,1,0:T(8,128)(2,1)S(1)}, bf16[4,8,256,128]{3,2,1,0:T(8,128)(2,1)S(1)}, f32[4,8,128,128]{3,2,1,0:T(8,128)S(1)}) custom-call(f32[14,1024]{1,0:T(8,128)S(1)} %fusion.lam_ref, bf16[4,8,256,128]{3,2,1,0:T(8,128)(2,1)S(1)} %get-tuple-element.45.k_ref, ...), custom_call_target="tpu_custom_call" | custom-call | flops 3758096384 | bytes 4194304 | tf_op jit(solution)/shard_map/local/pallas_call | solution.py:442
  30.1 0.0 collective-permute-done.4.refs_0_
  30.1 0.8 %collective-permute-done.5.refs_1_ = f32[4,128,128]{2,1,0:T(8,128)S(1)} collective-permute-done((f32[4,128,128]{2,1,0:T(8,128)S(1)}, f32[4,128,128]{2,1,0:T(8,128)S(1)}, u32[]{:S(2)}, u32[]{:S(2)}) %collective-permute-start.5) | collective-permute-done | bytes 262176 | tf_op jit(solution)/shard_map/ppermute | solution.py:342
  30.9 1.4 %collective-permute-done.6.refs_2_ = f32[4,128,128]{2,1,0:T(8,128)S(1)} collective-permute-done((f32[4,128,128]{2,1,0:T(8,128)S(1)}, f32[4,128,128]{2,1,0:T(8,128)S(1)}, u32[]{:S(2)}, u32[]{:S(2)}) %collective-permute-start.6) | collective-permute-done | bytes 262176 | tf_op jit(solution)/shard_map/ppermute | solution.py:342
  32.3 0.1 collective-permute-start.8
  32.4 1.3 %own_half.1 = (bf16[4,8,256,128]{3,2,1,0:T(8,128)(2,1)S(1)}, bf16[4,8,256,128]{3,2,1,0:T(8,128)(2,1)S(1)}, bf16[4,8,256,128]{3,2,1,0:T(8,128)(2,1)S(1)}) custom-call(f32[14,1024]{1,0:T(8,128)S(1)} %fusion.lam_ref, bf16[4,8,256,128]{3,2,1,0:T(8,128)(2,1)S(1)} %get-tuple-element.45.k_ref, ...), custom_call_target="tpu_custom_call", output_to_operand_aliasing={{0}: (6, {}), {1}: (7, {}), {2}: (8, {})} | custom-call | flops 671088640 | bytes 8388608 | tf_op jit(solution)/shard_map/own_half/pallas_call | solution.py:471
  33.7 0.6 %collective-permute-done.8.sums_ref = f32[2,4,128,128]{3,2,1,0:T(8,128)S(1)} collective-permute-done((f32[2,4,128,128]{3,2,1,0:T(8,128)S(1)}, f32[2,4,128,128]{3,2,1,0:T(8,128)S(1)}, u32[]{:S(2)}, u32[]{:S(2)}) %collective-permute-start.8) | collective-permute-done | bytes 524320 | tf_op jit(solution)/shard_map/ppermute | solution.py:342
  34.3 4.7 %final.1 = (bf16[1024,8,128]{2,1,0:T(8,128)(2,1)}, bf16[1024,8,128]{2,1,0:T(8,128)(2,1)}, bf16[1024,8,128]{2,1,0:T(8,128)(2,1)}) custom-call(f32[14,1024]{1,0:T(8,128)S(1)} %fusion.lam_ref, bf16[4,8,256,128]{3,2,1,0:T(8,128)(2,1)S(1)} %get-tuple-element.45.k_ref, bf16[4,8,256,128]{3,2,1,0:T(8,128)(2,1)S(1)} %get-tuple-element.46.v_ref, ...), custom_call_target="tpu_custom_call" | custom-call | flops 671088640 | bytes 16777216 | tf_op jit(solution)/shard_map/final/pallas_call | solution.py:483
  (4 shorter events, 0.1 us)
Async XLA Ops:
  0.6 11.2 %collective-permute-start = (s32[21,256]{1,0:T(8,128)}, s32[21,256]{1,0:T(8,128)S(1)}, u32[]{:S(2)}, u32[]{:S(2)}) collective-permute-start(s32[21,256]{1,0:T(8,128)} %param.9), channel_id=1, source_target_pairs={{0,1},{1,2},{2,3},{3,0},{4,5},{5,6},{6,7},{7,4},{8,9},{9,10},{10,1... | collective-permute-start | bytes 64520 | tf_op jit(solution)/shard_map/ppermute | solution.py:391
  3.7 8.1 %collective-permute-start.2 = (s32[21,256]{1,0:T(8,128)}, s32[21,256]{1,0:T(8,128)S(1)}, u32[]{:S(2)}, u32[]{:S(2)}) collective-permute-start(s32[21,256]{1,0:T(8,128)} %param.9), channel_id=1, source_target_pairs={{0,3},{1,0},{2,1},{3,2},{4,7},{5,4},{6,5},{7,6},{8,11},{9,8},{10,9... | collective-permute-start | bytes 64520 | tf_op jit(solution)/shard_map/ppermute | solution.py:391
  5.8 6.0 %collective-permute-start.1 = (s32[21,256]{1,0:T(8,128)}, s32[21,256]{1,0:T(8,128)S(1)}, u32[]{:S(2)}, u32[]{:S(2)}) collective-permute-start(s32[21,256]{1,0:T(8,128)} %param.9), channel_id=1, source_target_pairs={{0,2},{1,3},{2,0},{3,1},{4,6},{5,7},{6,4},{7,5},{8,10},{9,11},{10,... | collective-permute-start | bytes 64520 | tf_op jit(solution)/shard_map/ppermute | solution.py:391
  6.8 5.1 %copy-start = (s32[21,256]{1,0:T(8,128)S(1)}, s32[21,256]{1,0:T(8,128)}, u32[]{:S(2)}) copy-start(s32[21,256]{1,0:T(8,128)} %param.9) | copy-start | bytes 64516
  13.0 2.4 %collective-permute-start.3 = (f32[12,128,128]{2,1,0:T(8,128)S(1)}, f32[12,128,128]{2,1,0:T(8,128)S(1)}, u32[]{:S(2)}, u32[]{:S(2)}) collective-permute-start(f32[12,128,128]{2,1,0:T(8,128)S(1)} %get-tuple-element.52), channel_id=1, source_target_pairs={{0,4},{4,0},{8,12},{12,8},{16,20},{20,16},{24,28},{28,24},{1,5},{5... | collective-permute-start | bytes 2359304 | tf_op jit(solution)/shard_map/ppermute | solution.py:342
  15.4 3.7 %collective-permute-start.7 = (f32[8,128,128]{2,1,0:T(8,128)S(1)}, f32[8,128,128]{2,1,0:T(8,128)S(1)}, u32[]{:S(2)}, u32[]{:S(2)}) collective-permute-start(f32[8,128,128]{2,1,0:T(8,128)S(1)} %get-tuple-element.61), channel_id=1, source_target_pairs={{0,4},{4,0},{8,12},{12,8},{16,20},{20,16},{24,28},{28,24},{1,5},{5... | collective-permute-start | bytes 1572872 | tf_op jit(solution)/shard_map/ppermute | solution.py:342
  15.6 14.5 %collective-permute-start.4 = (f32[4,128,128]{2,1,0:T(8,128)S(1)}, f32[4,128,128]{2,1,0:T(8,128)S(1)}, u32[]{:S(2)}, u32[]{:S(2)}) collective-permute-start(f32[4,128,128]{2,1,0:T(8,128)S(1)} %get-tuple-element.57), channel_id=1, source_target_pairs={{0,8},{4,12},{8,0},{12,4},{16,24},{20,28},{24,16},{28,20},{1,9},{5... | collective-permute-start | bytes 786440 | tf_op jit(solution)/shard_map/ppermute | solution.py:342
  17.1 13.8 %collective-permute-start.5 = (f32[4,128,128]{2,1,0:T(8,128)S(1)}, f32[4,128,128]{2,1,0:T(8,128)S(1)}, u32[]{:S(2)}, u32[]{:S(2)}) collective-permute-start(f32[4,128,128]{2,1,0:T(8,128)S(1)} %get-tuple-element.58), channel_id=1, source_target_pairs={{0,24},{4,28},{8,16},{12,20},{16,8},{20,12},{24,0},{28,4},{1,25},{... | collective-permute-start | bytes 786440 | tf_op jit(solution)/shard_map/ppermute | solution.py:342
  18.6 13.6 %collective-permute-start.6 = (f32[4,128,128]{2,1,0:T(8,128)S(1)}, f32[4,128,128]{2,1,0:T(8,128)S(1)}, u32[]{:S(2)}, u32[]{:S(2)}) collective-permute-start(f32[4,128,128]{2,1,0:T(8,128)S(1)} %get-tuple-element.59), channel_id=1, source_target_pairs={{0,16},{4,20},{8,24},{12,28},{16,0},{20,4},{24,8},{28,12},{1,17},{... | collective-permute-start | bytes 786440 | tf_op jit(solution)/shard_map/ppermute | solution.py:342
  32.3 2.0 %collective-permute-start.8 = (f32[2,4,128,128]{3,2,1,0:T(8,128)S(1)}, f32[2,4,128,128]{3,2,1,0:T(8,128)S(1)}, u32[]{:S(2)}, u32[]{:S(2)}) collective-permute-start(f32[2,4,128,128]{3,2,1,0:T(8,128)S(1)} %sums.1.sums_ref), channel_id=1, source_target_pairs={{0,4},{4,0},{8,12},{12,8},{16,20},{20,16},{24,28},{28,24},{1,5},{5... | collective-permute-start | bytes 1572872 | tf_op jit(solution)/shard_map/ppermute | solution.py:342

commit v3 on v1

--- a/solution.py
+++ b/solution.py
@@ -255,7 +255,7 @@
 
 def final_kernel(
     first_row, lam_ref, k_ref, v_ref, g_ref, dq_in, dk_in, dv_in, gin_ref, sums_ref,
-    dq_out, dk_out, dv_out, done_ref, wide_ref, half_ref, state_ref, sems,
+    dq_out, dk_out, dv_out, done_ref, heads_ref, wide_ref, half_ref, state_ref, sems,
 ):
     chunks, heads, tile, _ = k_ref.shape
     half = half_ref.shape[0]
@@ -282,7 +282,7 @@
         def _():
             for c in range(chunks):
                 widen(lam_ref, first_row, slice(c * tile, (c + 1) * tile), wide_ref)
-                queries, keys, values = [], [], []
+                slot = c % 2
                 for h in range(heads):
                     query, key, value = dq_in[c, h], dk_in[c, h], dv_in[c, h]
                     if h // half != core:
@@ -291,11 +291,10 @@
                         key, value = add_to_key_value(
                             gin_ref[c, h] + state_ref[i], k_ref[c, h], v_ref[c, h], key, value
                         )
-                    queries.append(query)
-                    keys.append(key)
-                    values.append(value)
-                for n, parts in enumerate((queries, keys, values)):
-                    done_ref[n, c] = jnp.swapaxes(jnp.stack(parts), 0, 1)
+                    for n, part in enumerate((query, key, value)):
+                        heads_ref[slot, n, h] = part
+                for n in range(3):
+                    done_ref[n, c] = jnp.swapaxes(heads_ref[slot, n], 0, 1)
                     for copy in ship(n, c):
                         copy.start()
 
@@ -478,10 +477,11 @@
         out_specs=[anywhere] * 3,
         out_shape=[pltpu.HBM((count, heads, width), BF16)] * 3,
         scratch_shapes=[
-            pltpu.VMEM((3, chunks, tile, heads, width), BF16), *kept,
+            pltpu.VMEM((3, chunks, tile, heads, width), BF16),
+            pltpu.VMEM((2, 3, heads, tile, width), BF16), *kept,
             pltpu.SemaphoreType.DMA((3, chunks, pieces)),
         ],
-        compiler_params=params(10),
+        compiler_params=params(14),
         cost_estimate=cost((tree_bits + 2) * size * width, 16 * size),
         name="final",
     )(lam, kh, vh, gh, *near(*parts), gin, others)

time: 37.9 us -> 38.6 us (1.018)
  Pallas kernels: 24.2 us -> 24.8 us
    pallas_call x1, Pallas kernels: 4.74 us -> 5.43 us  [on_device(): pl.pallas_call(functools.partial(final_kernel, local_bits + 2), in_specs=...]
  transfers between devices with their start and end apart: 9 -> 9, of which waited for: 3 -> 3; matrix products, arithmetic and copies ran while one was open for 0% -> 0% of each run, Pallas kernels for 49% -> 48%
where the time goes in v3:
time: 38.6 us; the launch traced here: 38.4 us
  Pallas kernels  24.8 us (64%)
  starting transfers between devices  9.96 us (26%)
  waiting for transfers between devices  2.54 us (7%)
  between operations  0.95 us (2%)
    pallas_call x1, Pallas kernels, on_device(): pl.pallas_call(local_kernel, in_specs=[in_vmem] * 7, out_specs=[in_vmem]...  11 us
    ppermute x3, starting transfers between devices, on_device(): lax.ppermute(level_codes, 'head', [(i, (i + r) % groups) for i in range(g...  6.11 us
    pallas_call x1, Pallas kernels, on_device(): pl.pallas_call(functools.partial(final_kernel, local_bits + 2), in_specs=...  5.43 us
    pallas_call x1, Pallas kernels, on_device(): pl.pallas_call(functools.partial(states_kernel, pieces), grid=(chunks,),...  5 us
    ppermute x6, starting transfers between devices, permute(): return lax.ppermute(x, 'seq', [(i, i ^ apart) for i in range(blocks)])  3.85 us
    ppermute x6, waiting for transfers between devices, permute(): return lax.ppermute(x, 'seq', [(i, i ^ apart) for i in range(blocks)])  2.54 us
    pallas_call x2, Pallas kernels, level_grads(): pl.pallas_call(functools.partial(grads_kernel, local_bits + 1, own), in_s...  1.99 us
    pallas_call x1, Pallas kernels, on_device(): pl.pallas_call(functools.partial(own_half_kernel, local_bits + 2), in_spe...  1.34 us
  transfers between devices with their start and end apart: 9, of which 3 were waited for; matrix products, arithmetic and copies ran while one was open for 0% of the time, Pallas kernels for 48%

profile of v3, /device:TPU:0, one launch (start us, length us, event | category | flops | bytes accessed | tf_op | source)
XLA Modules:
  0.0 38.4 jit_solution(17919126307524304539)
XLA Ops:
  0.6 3.1 %collective-permute-start = (s32[21,256]{1,0:T(8,128)}, s32[21,256]{1,0:T(8,128)S(1)}, u32[]{:S(2)}, u32[]{:S(2)}) collective-permute-start(s32[21,256]{1,0:T(8,128)} %param.9), channel_id=1, source_target_pairs={{0,1},{1,2},{2,3},{3,0},{4,5},{5,6},{6,7},{7,4},{8,9},{9,10},{10,1... | collective-permute-start | bytes 64520 | tf_op jit(solution)/shard_map/ppermute | solution.py:382
  3.7 2.1 %collective-permute-start.2 = (s32[21,256]{1,0:T(8,128)}, s32[21,256]{1,0:T(8,128)S(1)}, u32[]{:S(2)}, u32[]{:S(2)}) collective-permute-start(s32[21,256]{1,0:T(8,128)} %param.9), channel_id=1, source_target_pairs={{0,3},{1,0},{2,1},{3,2},{4,7},{5,4},{6,5},{7,6},{8,11},{9,8},{10,9... | collective-permute-start | bytes 64520 | tf_op jit(solution)/shard_map/ppermute | solution.py:382
  5.8 0.9 %collective-permute-start.1 = (s32[21,256]{1,0:T(8,128)}, s32[21,256]{1,0:T(8,128)S(1)}, u32[]{:S(2)}, u32[]{:S(2)}) collective-permute-start(s32[21,256]{1,0:T(8,128)} %param.9), channel_id=1, source_target_pairs={{0,2},{1,3},{2,0},{3,1},{4,6},{5,7},{6,4},{7,5},{8,10},{9,11},{10,... | collective-permute-start | bytes 64520 | tf_op jit(solution)/shard_map/ppermute | solution.py:382
  6.8 0.0 copy-start
  6.8 5.0 %states.1 = (bf16[4,8,256,128]{3,2,1,0:T(8,128)(2,1)S(1)}, bf16[4,8,256,128]{3,2,1,0:T(8,128)(2,1)S(1)}, bf16[4,8,256,128]{3,2,1,0:T(8,128)(2,1)S(1)}, bf16[4,8,...) custom-call(bf16[1024,8,128]{2,1,0:T(8,128)(2,1)} %refs_1_.1, ...), custom_call_target="tpu_custom_call" | custom-call | flops 268435456 | bytes 8388608 | tf_op jit(solution)/shard_map/states/pallas_call | solution.py:358
  11.8 0.0 collective-permute-done
  11.8 0.0 collective-permute-done.2
  11.8 0.0 collective-permute-done.1
  11.8 0.0 copy-done
  11.9 0.1 fusion.lam_ref
  12.0 1.0 %level_grads.2 = (f32[12,128,128]{2,1,0:T(8,128)S(1)}, f32[8,128,128]{2,1,0:T(8,128)S(1)}) custom-call(f32[14,1024]{1,0:T(8,128)S(1)} %fusion.lam_ref, bf16[4,8,128,256]{3,2,1,0:T(8,128)(2,1)S(1)} %get-tuple-element.48.qt_ref, bf16[4,8,256,128]{3,2,1,0:T(8,128)(2,1)S(1)} %get-tuple-element.47.g_ref, f32[8,128,128]{2,1,0:T(8,128)S(1)} %get-tuple-element.49.state_ref), custom_call_target="tpu_custom_call" | custom-call | flops 402653184 | bytes 1048576 | tf_op jit(solution)/shard_map/level_grads/pallas_call | solution.py:404
  13.0 0.1 collective-permute-start.3
  13.0 1.0 %level_grads.3 = (f32[12,128,128]{2,1,0:T(8,128)S(1)}, f32[8,128,128]{2,1,0:T(8,128)S(1)}) custom-call(f32[14,1024]{1,0:T(8,128)S(1)} %fusion.lam_ref, bf16[4,8,128,256]{3,2,1,0:T(8,128)(2,1)S(1)} %get-tuple-element.48.qt_ref, bf16[4,8,256,128]{3,2,1,0:T(8,128)(2,1)S(1)} %get-tuple-element.47.g_ref, ...), custom_call_target="tpu_custom_call", output_to_operand_aliasing={{1}: (4, {})} | custom-call | flops 402653184 | bytes 1048576 | tf_op jit(solution)/shard_map/level_grads/pallas_call | solution.py:404
  14.0 1.3 %collective-permute-done.3.found_ref = f32[12,128,128]{2,1,0:T(8,128)S(1)} collective-permute-done((f32[12,128,128]{2,1,0:T(8,128)S(1)}, f32[12,128,128]{2,1,0:T(8,128)S(1)}, u32[]{:S(2)}, u32[]{:S(2)}) %collective-permute-start.3) | collective-permute-done | bytes 786464 | tf_op jit(solution)/shard_map/ppermute | solution.py:333
  15.3 0.1 pair.1
  15.4 0.2 collective-permute-start.7
  15.6 2.5 %collective-permute-start.4 = (f32[4,128,128]{2,1,0:T(8,128)S(1)}, f32[4,128,128]{2,1,0:T(8,128)S(1)}, u32[]{:S(2)}, u32[]{:S(2)}) collective-permute-start(f32[4,128,128]{2,1,0:T(8,128)S(1)} %get-tuple-element.57), channel_id=1, source_target_pairs={{0,24},{4,28},{8,16},{12,20},{16,8},{20,12},{24,0},{28,4},{1,25},{... | collective-permute-start | bytes 786440 | tf_op jit(solution)/shard_map/ppermute | solution.py:333
  18.1 0.5 %collective-permute-start.5 = (f32[4,128,128]{2,1,0:T(8,128)S(1)}, f32[4,128,128]{2,1,0:T(8,128)S(1)}, u32[]{:S(2)}, u32[]{:S(2)}) collective-permute-start(f32[4,128,128]{2,1,0:T(8,128)S(1)} %get-tuple-element.58), channel_id=1, source_target_pairs={{0,8},{4,12},{8,0},{12,4},{16,24},{20,28},{24,16},{28,20},{1,9},{5... | collective-permute-start | bytes 786440 | tf_op jit(solution)/shard_map/ppermute | solution.py:333
  18.6 0.5 %collective-permute-start.6 = (f32[4,128,128]{2,1,0:T(8,128)S(1)}, f32[4,128,128]{2,1,0:T(8,128)S(1)}, u32[]{:S(2)}, u32[]{:S(2)}) collective-permute-start(f32[4,128,128]{2,1,0:T(8,128)S(1)} %get-tuple-element.59), channel_id=1, source_target_pairs={{0,16},{4,20},{8,24},{12,28},{16,0},{20,4},{24,8},{28,12},{1,17},{... | collective-permute-start | bytes 786440 | tf_op jit(solution)/shard_map/ppermute | solution.py:333
  19.1 0.0 collective-permute-done.7.found_ref
  19.1 11.0 %local.1 = (bf16[4,8,256,128]{3,2,1,0:T(8,128)(2,1)S(1)}, bf16[4,8,256,128]{3,2,1,0:T(8,128)(2,1)S(1)}, bf16[4,8,256,128]{3,2,1,0:T(8,128)(2,1)S(1)}, f32[4,8,128,128]{3,2,1,0:T(8,128)S(1)}) custom-call(f32[14,1024]{1,0:T(8,128)S(1)} %fusion.lam_ref, bf16[4,8,256,128]{3,2,1,0:T(8,128)(2,1)S(1)} %get-tuple-element.45.k_ref, ...), custom_call_target="tpu_custom_call" | custom-call | flops 3758096384 | bytes 4194304 | tf_op jit(solution)/shard_map/local/pallas_call | solution.py:433
  30.1 0.0 collective-permute-done.4.refs_0_
  30.1 0.7 %collective-permute-done.5.refs_1_ = f32[4,128,128]{2,1,0:T(8,128)S(1)} collective-permute-done((f32[4,128,128]{2,1,0:T(8,128)S(1)}, f32[4,128,128]{2,1,0:T(8,128)S(1)}, u32[]{:S(2)}, u32[]{:S(2)}) %collective-permute-start.5) | collective-permute-done | bytes 262176 | tf_op jit(solution)/shard_map/ppermute | solution.py:333
  30.8 0.0 collective-permute-done.6.refs_2_
  30.9 0.1 collective-permute-start.8
  30.9 1.3 %own_half.1 = (bf16[4,8,256,128]{3,2,1,0:T(8,128)(2,1)S(1)}, bf16[4,8,256,128]{3,2,1,0:T(8,128)(2,1)S(1)}, bf16[4,8,256,128]{3,2,1,0:T(8,128)(2,1)S(1)}) custom-call(f32[14,1024]{1,0:T(8,128)S(1)} %fusion.lam_ref, bf16[4,8,256,128]{3,2,1,0:T(8,128)(2,1)S(1)} %get-tuple-element.45.k_ref, ...), custom_call_target="tpu_custom_call", output_to_operand_aliasing={{0}: (6, {}), {1}: (7, {}), {2}: (8, {})} | custom-call | flops 671088640 | bytes 8388608 | tf_op jit(solution)/shard_map/own_half/pallas_call | solution.py:462
  32.3 0.6 %collective-permute-done.8.sums_ref = f32[2,4,128,128]{3,2,1,0:T(8,128)S(1)} collective-permute-done((f32[2,4,128,128]{3,2,1,0:T(8,128)S(1)}, f32[2,4,128,128]{3,2,1,0:T(8,128)S(1)}, u32[]{:S(2)}, u32[]{:S(2)}) %collective-permute-start.8) | collective-permute-done | bytes 524320 | tf_op jit(solution)/shard_map/ppermute | solution.py:333
  32.8 5.4 %final.1 = (bf16[1024,8,128]{2,1,0:T(8,128)(2,1)}, bf16[1024,8,128]{2,1,0:T(8,128)(2,1)}, bf16[1024,8,128]{2,1,0:T(8,128)(2,1)}) custom-call(f32[14,1024]{1,0:T(8,128)S(1)} %fusion.lam_ref, bf16[4,8,256,128]{3,2,1,0:T(8,128)(2,1)S(1)} %get-tuple-element.45.k_ref, bf16[4,8,256,128]{3,2,1,0:T(8,128)(2,1)S(1)} %get-tuple-element.46.v_ref, ...), custom_call_target="tpu_custom_call" | custom-call | flops 671088640 | bytes 16777216 | tf_op jit(solution)/shard_map/final/pallas_call | solution.py:474
  (4 shorter events, 0.1 us)
Async XLA Ops:
  0.6 11.2 %collective-permute-start = (s32[21,256]{1,0:T(8,128)}, s32[21,256]{1,0:T(8,128)S(1)}, u32[]{:S(2)}, u32[]{:S(2)}) collective-permute-start(s32[21,256]{1,0:T(8,128)} %param.9), channel_id=1, source_target_pairs={{0,1},{1,2},{2,3},{3,0},{4,5},{5,6},{6,7},{7,4},{8,9},{9,10},{10,1... | collective-permute-start | bytes 64520 | tf_op jit(solution)/shard_map/ppermute | solution.py:382
  3.7 8.1 %collective-permute-start.2 = (s32[21,256]{1,0:T(8,128)}, s32[21,256]{1,0:T(8,128)S(1)}, u32[]{:S(2)}, u32[]{:S(2)}) collective-permute-start(s32[21,256]{1,0:T(8,128)} %param.9), channel_id=1, source_target_pairs={{0,3},{1,0},{2,1},{3,2},{4,7},{5,4},{6,5},{7,6},{8,11},{9,8},{10,9... | collective-permute-start | bytes 64520 | tf_op jit(solution)/shard_map/ppermute | solution.py:382
  5.8 6.0 %collective-permute-start.1 = (s32[21,256]{1,0:T(8,128)}, s32[21,256]{1,0:T(8,128)S(1)}, u32[]{:S(2)}, u32[]{:S(2)}) collective-permute-start(s32[21,256]{1,0:T(8,128)} %param.9), channel_id=1, source_target_pairs={{0,2},{1,3},{2,0},{3,1},{4,6},{5,7},{6,4},{7,5},{8,10},{9,11},{10,... | collective-permute-start | bytes 64520 | tf_op jit(solution)/shard_map/ppermute | solution.py:382
  6.8 5.1 %copy-start = (s32[21,256]{1,0:T(8,128)S(1)}, s32[21,256]{1,0:T(8,128)}, u32[]{:S(2)}) copy-start(s32[21,256]{1,0:T(8,128)} %param.9) | copy-start | bytes 64516
  13.0 2.4 %collective-permute-start.3 = (f32[12,128,128]{2,1,0:T(8,128)S(1)}, f32[12,128,128]{2,1,0:T(8,128)S(1)}, u32[]{:S(2)}, u32[]{:S(2)}) collective-permute-start(f32[12,128,128]{2,1,0:T(8,128)S(1)} %get-tuple-element.52), channel_id=1, source_target_pairs={{0,4},{4,0},{8,12},{12,8},{16,20},{20,16},{24,28},{28,24},{1,5},{5... | collective-permute-start | bytes 2359304 | tf_op jit(solution)/shard_map/ppermute | solution.py:333
  15.4 3.7 %collective-permute-start.7 = (f32[8,128,128]{2,1,0:T(8,128)S(1)}, f32[8,128,128]{2,1,0:T(8,128)S(1)}, u32[]{:S(2)}, u32[]{:S(2)}) collective-permute-start(f32[8,128,128]{2,1,0:T(8,128)S(1)} %get-tuple-element.61), channel_id=1, source_target_pairs={{0,4},{4,0},{8,12},{12,8},{16,20},{20,16},{24,28},{28,24},{1,5},{5... | collective-permute-start | bytes 1572872 | tf_op jit(solution)/shard_map/ppermute | solution.py:333
  15.6 14.5 %collective-permute-start.4 = (f32[4,128,128]{2,1,0:T(8,128)S(1)}, f32[4,128,128]{2,1,0:T(8,128)S(1)}, u32[]{:S(2)}, u32[]{:S(2)}) collective-permute-start(f32[4,128,128]{2,1,0:T(8,128)S(1)} %get-tuple-element.57), channel_id=1, source_target_pairs={{0,24},{4,28},{8,16},{12,20},{16,8},{20,12},{24,0},{28,4},{1,25},{... | collective-permute-start | bytes 786440 | tf_op jit(solution)/shard_map/ppermute | solution.py:333
  18.1 12.7 %collective-permute-start.5 = (f32[4,128,128]{2,1,0:T(8,128)S(1)}, f32[4,128,128]{2,1,0:T(8,128)S(1)}, u32[]{:S(2)}, u32[]{:S(2)}) collective-permute-start(f32[4,128,128]{2,1,0:T(8,128)S(1)} %get-tuple-element.58), channel_id=1, source_target_pairs={{0,8},{4,12},{8,0},{12,4},{16,24},{20,28},{24,16},{28,20},{1,9},{5... | collective-permute-start | bytes 786440 | tf_op jit(solution)/shard_map/ppermute | solution.py:333
  18.6 12.2 %collective-permute-start.6 = (f32[4,128,128]{2,1,0:T(8,128)S(1)}, f32[4,128,128]{2,1,0:T(8,128)S(1)}, u32[]{:S(2)}, u32[]{:S(2)}) collective-permute-start(f32[4,128,128]{2,1,0:T(8,128)S(1)} %get-tuple-element.59), channel_id=1, source_target_pairs={{0,16},{4,20},{8,24},{12,28},{16,0},{20,4},{24,8},{28,12},{1,17},{... | collective-permute-start | bytes 786440 | tf_op jit(solution)/shard_map/ppermute | solution.py:333
  30.9 2.0 %collective-permute-start.8 = (f32[2,4,128,128]{3,2,1,0:T(8,128)S(1)}, f32[2,4,128,128]{3,2,1,0:T(8,128)S(1)}, u32[]{:S(2)}, u32[]{:S(2)}) collective-permute-start(f32[2,4,128,128]{3,2,1,0:T(8,128)S(1)} %sums.1.sums_ref), channel_id=1, source_target_pairs={{0,4},{4,0},{8,12},{12,8},{16,20},{20,16},{24,28},{28,24},{1,5},{5... | collective-permute-start | bytes 1572872 | tf_op jit(solution)/shard_map/ppermute | solution.py:333

commit v4 on v1

--- a/solution.py
+++ b/solution.py
@@ -46,7 +46,8 @@
 
 def states_kernel(pieces, *refs):
     inputs = [refs[n * pieces : (n + 1) * pieces] for n in range(4)]
-    kh_ref, vh_ref, gh_ref, qt_ref, level_ref, total_ref, chunk_ref = refs[4 * pieces :]
+    kh_ref, vh_ref, gh_ref, qt_ref, level_ref, total_ref, send_ref, chunk_ref = refs[4 * pieces :]
+    half = send_ref.shape[0]
     heads = kh_ref.shape[1]
     size = kh_ref.shape[2] // pieces
     chunks = chunk_ref.shape[0]
@@ -70,6 +71,12 @@
             for n, sources in enumerate(level_sources(chunks)):
                 state = functools.reduce(jnp.add, [tiles[i] for i in sources])
                 level_ref[n, h] = state.astype(BF16)
+        for core in range(2):
+
+            @pl.when(bit_of_block(0) == core)
+            def _():
+                for i in range(half):
+                    send_ref[i] = total_ref[(1 - core) * half + i]
 
 
 def grads_kernel(first_row, own, lam_ref, qt_ref, g_ref, state_ref, *refs):
@@ -100,9 +107,8 @@
                 ]
                 grad = dot(stack_levels(weighted, 1), g_ref[:, h].reshape(chunks * tile, width))
                 parts = [grad[b * width : (b + 1) * width] for b in range(levels)]
-                state = state_ref[h]
-                whole_ref[h] = state if core == 0 else parts[0]
-                for b, part in enumerate([state, *parts[1:]]):
+                whole_ref[h] = state_ref[h] if core == 0 else parts[0]
+                for b, part in enumerate(parts[1:]):
                     sums_ref[b * half + h % half] = part
 
 
@@ -175,16 +181,20 @@
             dq_ref[c, h] = dqt.astype(BF16).T
 
 
-def pair_kernel(levels, keep_ref, found_ref, *out_refs):
+def pair_kernel(levels, state_ref, other_ref, keep_ref, found_ref, *out_refs):
     half = out_refs[0].shape[0]
+    start = bit_of_block(0) * half
     for b, out_ref in zip(levels, out_refs):
         for on in range(2):
 
             @pl.when(bit_of_block(b) == on)
             def _():
                 for i in range(half):
-                    spot = b * on * half + i
-                    out_ref[i] = keep_ref[spot] + found_ref[spot]
+                    if on:
+                        spot = (b - 1) * half + i
+                        out_ref[i] = keep_ref[spot] + found_ref[spot]
+                    else:
+                        out_ref[i] = state_ref[start + i] + other_ref[i]
 
 
 def sum_kernel(levels, *refs):
@@ -356,7 +366,7 @@
     groups_in = len(level_sources(chunks))
     queries, keys, values, out_grad = in_hbm(queries, keys, values, out_grad)
 
-    kh, vh, gh, qt, level_state, state = pl.pallas_call(
+    kh, vh, gh, qt, level_state, state, send_state = pl.pallas_call(
         functools.partial(states_kernel, pieces),
         grid=(chunks,),
         in_specs=[
@@ -366,17 +376,20 @@
         ],
         out_specs=[
             *[head_block] * 3, chunk_block(heads, width, tile),
-            whole(groups_in, heads, *square), whole(heads, *square),
+            whole(groups_in, heads, *square), whole(heads, *square), whole(half, *square),
         ],
         out_shape=[
             *[natural] * 3, pltpu.VMEM((chunks, heads, width, tile), BF16),
             pltpu.VMEM((groups_in, heads, *square), BF16), pltpu.VMEM((heads, *square), F32),
+            pltpu.VMEM((half, *square), F32),
         ],
         scratch_shapes=[pltpu.VMEM((chunks, heads, *square), F32)],
         compiler_params=params(8),
         cost_estimate=cost(2 * size * width, 8 * size),
         name="states",
     )(*[x for x in (keys, values, queries, out_grad) for _ in range(pieces)])
+
+    other_state = permute(send_state, 1)
 
     group = lax.axis_index("head")
     parts = [
@@ -406,7 +419,7 @@
             functools.partial(grads_kernel, local_bits + 1, own),
             in_specs=[in_vmem] * len(inputs) + [anywhere] * len(before),
             out_specs=[in_vmem] * 2,
-            out_shape=[pltpu.VMEM((n, *square), F32) for n in (tree_bits * half, heads)],
+            out_shape=[pltpu.VMEM((n, *square), F32) for n in ((tree_bits - 1) * half, heads)],
             input_output_aliases={len(inputs): 1} if before else {},
             compiler_params=params(4),
             cost_estimate=cost(tree_bits * size * width, size),
@@ -414,6 +427,7 @@
         )(*inputs, *before)
 
     send, everything = level_grads(False, [])
+    send, other_state = lax.optimization_barrier((send, other_state))
     found = permute(send, 1)
     keep, everything = level_grads(True, near(everything))
     (keep,) = near(keep)
@@ -421,13 +435,13 @@
     hops.sort(key=lambda hop: (hop & hop - 1) == 0)
     messages = pl.pallas_call(
         functools.partial(pair_kernel, [bits_of(hop) for hop in hops]),
-        in_specs=[in_vmem] * 2,
+        in_specs=[in_vmem] * 4,
         out_specs=[in_vmem] * len(hops),
         out_shape=[pltpu.VMEM((half, *square), F32)] * len(hops),
         compiler_params=params(2),
         cost_estimate=cost(size, size),
         name="pair",
-    )(keep, found)
+    )(state, other_state, keep, found)
     *messages, everything = lax.optimization_barrier((*messages, everything))
     arrived = [permute(x, hop) for hop, x in zip(hops, messages)]
     first = permute(everything, 1)

time: 37.9 us -> 44.2 us (1.17)
  local copies, waits for them, and re-layouts: 0.03 us -> 6.47 us
  waiting for transfers between devices: 2.54 us -> 1.54 us
  starting transfers between devices: 9.96 us -> 10.7 us
    unnamed x2 -> x20, local copies, waits for them, and re-layouts: 0.01 us -> 6.45 us
    ppermute x6 -> x7, waiting for transfers between devices: 2.54 us -> 1.53 us  [permute(): return lax.ppermute(x, 'seq', [(i, i ^ apart) for i in range(blocks)])]
    ppermute x6 -> x7, starting transfers between devices: 3.85 us -> 4.56 us  [permute(): return lax.ppermute(x, 'seq', [(i, i ^ apart) for i in range(blocks)])]
  transfers between devices with their start and end apart: 9 -> 10, of which waited for: 3 -> 3; matrix products, arithmetic and copies ran while one was open for 0% -> 0% of each run, Pallas kernels for 49% -> 44%
where the time goes in v4:
time: 44.2 us; the launch traced here: 44 us
  Pallas kernels  24.2 us (55%)
  starting transfers between devices  10.7 us (24%)
  local copies, waits for them, and re-layouts  6.47 us (15%)
  waiting for transfers between devices  1.54 us (3%)
  between operations  1.04 us (2%)
    pallas_call x1, Pallas kernels, on_device(): pl.pallas_call(local_kernel, in_specs=[in_vmem] * 7, out_specs=[in_vmem]...  11 us
    unnamed x20, local copies, waits for them, and re-layouts  6.45 us
    ppermute x3, starting transfers between devices, on_device(): lax.ppermute(level_codes, 'head', [(i, (i + r) % groups) for i in range(g...  6.11 us
    pallas_call x1, Pallas kernels, on_device(): pl.pallas_call(functools.partial(states_kernel, pieces), grid=(chunks,),...  4.98 us
    pallas_call x1, Pallas kernels, on_device(): pl.pallas_call(functools.partial(final_kernel, local_bits + 2), in_specs=...  4.74 us
    ppermute x7, starting transfers between devices, permute(): return lax.ppermute(x, 'seq', [(i, i ^ apart) for i in range(blocks)])  4.56 us
    pallas_call x2, Pallas kernels, level_grads(): pl.pallas_call(functools.partial(grads_kernel, local_bits + 1, own), in_s...  1.98 us
    ppermute x7, waiting for transfers between devices, permute(): return lax.ppermute(x, 'seq', [(i, i ^ apart) for i in range(blocks)])  1.53 us
  transfers between devices with their start and end apart: 10, of which 3 were waited for; matrix products, arithmetic and copies ran while one was open for 0% of the time, Pallas kernels for 44%

profile of v4, /device:TPU:0, one launch (start us, length us, event | category | flops | bytes accessed | tf_op | source)
XLA Modules:
  0.0 44.0 jit_solution(18355178085917345837)
XLA Ops:
  0.6 0.0 copy-start.9
  0.6 3.1 %collective-permute-start = (s32[21,256]{1,0:T(8,128)}, s32[21,256]{1,0:T(8,128)S(1)}, u32[]{:S(2)}, u32[]{:S(2)}) collective-permute-start(s32[21,256]{1,0:T(8,128)} %param.9), channel_id=1, source_target_pairs={{0,1},{1,2},{2,3},{3,0},{4,5},{5,6},{6,7},{7,4},{8,9},{9,10},{10,1... | collective-permute-start | bytes 64520 | tf_op jit(solution)/shard_map/ppermute | solution.py:396
  3.7 2.1 %collective-permute-start.2 = (s32[21,256]{1,0:T(8,128)}, s32[21,256]{1,0:T(8,128)S(1)}, u32[]{:S(2)}, u32[]{:S(2)}) collective-permute-start(s32[21,256]{1,0:T(8,128)} %param.9), channel_id=1, source_target_pairs={{0,3},{1,0},{2,1},{3,2},{4,7},{5,4},{6,5},{7,6},{8,11},{9,8},{10,9... | collective-permute-start | bytes 64520 | tf_op jit(solution)/shard_map/ppermute | solution.py:396
  5.8 0.9 %collective-permute-start.1 = (s32[21,256]{1,0:T(8,128)}, s32[21,256]{1,0:T(8,128)S(1)}, u32[]{:S(2)}, u32[]{:S(2)}) collective-permute-start(s32[21,256]{1,0:T(8,128)} %param.9), channel_id=1, source_target_pairs={{0,2},{1,3},{2,0},{3,1},{4,6},{5,7},{6,4},{7,5},{8,10},{9,11},{10,... | collective-permute-start | bytes 64520 | tf_op jit(solution)/shard_map/ppermute | solution.py:396
  6.8 5.0 %states.1 = (bf16[4,8,256,128]{3,2,1,0:T(8,128)(2,1)S(1)}, bf16[4,8,256,128]{3,2,1,0:T(8,128)(2,1)S(1)}, bf16[4,8,256,128]{3,2,1,0:T(8,128)(2,1)S(1)}, bf16[4,8,...) custom-call(bf16[1024,8,128]{2,1,0:T(8,128)(2,1)} %refs_1_.1, ...), custom_call_target="tpu_custom_call" | custom-call | flops 268435456 | bytes 8388608 | tf_op jit(solution)/shard_map/states/pallas_call | solution.py:369
  11.7 0.0 copy-start
  11.8 1.3 %copy-done = bf16[4,8,128,256]{3,2,1,0:T(8,128)(2,1)} copy-done((bf16[4,8,128,256]{3,2,1,0:T(8,128)(2,1)}, bf16[4,8,128,256]{3,2,1,0:T(8,128)(2,1)S(1)}, u32[]{:S(2)}) %copy-start) | copy-done | bytes 2097176
  13.1 0.0 copy-start.3
  13.1 1.3 %copy-done.3 = bf16[4,8,256,128]{3,2,1,0:T(8,128)(2,1)} copy-done((bf16[4,8,256,128]{3,2,1,0:T(8,128)(2,1)}, bf16[4,8,256,128]{3,2,1,0:T(8,128)(2,1)S(1)}, u32[]{:S(2)}) %copy-start.3) | copy-done | bytes 2097176
  14.4 0.0 copy-start.5
  14.4 1.3 %copy-done.5 = bf16[4,8,256,128]{3,2,1,0:T(8,128)(2,1)} copy-done((bf16[4,8,256,128]{3,2,1,0:T(8,128)(2,1)}, bf16[4,8,256,128]{3,2,1,0:T(8,128)(2,1)S(1)}, u32[]{:S(2)}) %copy-start.5) | copy-done | bytes 2097176
  15.7 0.0 copy-start.7
  15.7 0.9 %copy-done.7 = bf16[3,8,128,128]{3,2,1,0:T(8,128)(2,1)} copy-done((bf16[3,8,128,128]{3,2,1,0:T(8,128)(2,1)}, bf16[3,8,128,128]{3,2,1,0:T(8,128)(2,1)S(1)}, u32[]{:S(2)}) %copy-start.7) | copy-done | bytes 786456
  16.6 0.0 collective-permute-start.3
  16.7 0.0 collective-permute-done
  16.7 0.0 collective-permute-done.2
  16.7 0.0 collective-permute-done.1
  16.7 0.0 copy-done.9
  16.8 0.1 fusion.lam_ref
  16.9 0.0 copy-start.1
  16.9 1.6 %copy-done.1 = bf16[4,8,128,256]{3,2,1,0:T(8,128)(2,1)S(1)} copy-done((bf16[4,8,128,256]{3,2,1,0:T(8,128)(2,1)S(1)}, bf16[4,8,128,256]{3,2,1,0:T(8,128)(2,1)}, u32[]{:S(2)}) %copy-start.1) | copy-done | bytes 2097176
  18.4 1.0 %level_grads.2 = (f32[8,128,128]{2,1,0:T(8,128)S(1)}, f32[8,128,128]{2,1,0:T(8,128)S(1)}) custom-call(f32[14,1024]{1,0:T(8,128)S(1)} %fusion.lam_ref, bf16[4,8,128,256]{3,2,1,0:T(8,128)(2,1)S(1)} %copy-done.1, bf16[4,8,256,128]{3,2,1,0:T(8,128)(2,1)S(1)} %get-tuple-element.50.g_ref, f32[8,128,128]{2,1,0:T(8,128)S(1)} %get-tuple-element.51.state_ref), custom_call_target="tpu_custom_call" | custom-call | flops 402653184 | bytes 1048576 | tf_op jit(solution)/shard_map/level_grads/pallas_call | solution.py:418
  19.4 0.0 collective-permute-done.3.other_ref
  19.4 0.6 %collective-permute-start.4 = (f32[8,128,128]{2,1,0:T(8,128)S(1)}, f32[8,128,128]{2,1,0:T(8,128)S(1)}, u32[]{:S(2)}, u32[]{:S(2)}) collective-permute-start(f32[8,128,128]{2,1,0:T(8,128)S(1)} %get-tuple-element.58), channel_id=1, source_target_pairs={{0,4},{4,0},{8,12},{12,8},{16,20},{20,16},{24,28},{28,24},{1,5},{5... | collective-permute-start | bytes 1572872 | tf_op jit(solution)/shard_map/ppermute | solution.py:344
  20.0 0.0 copy-start.2
  20.0 0.0 copy-start.4
  20.0 0.0 copy-start.6
  20.0 0.0 copy-start.8
  20.0 1.0 %level_grads.3 = (f32[8,128,128]{2,1,0:T(8,128)S(1)}, f32[8,128,128]{2,1,0:T(8,128)S(1)}) custom-call(f32[14,1024]{1,0:T(8,128)S(1)} %fusion.lam_ref, bf16[4,8,128,256]{3,2,1,0:T(8,128)(2,1)S(1)} %copy-done.1, bf16[4,8,256,128]{3,2,1,0:T(8,128)(2,1)S(1)} %get-tuple-element.50.g_ref, ...), custom_call_target="tpu_custom_call", output_to_operand_aliasing={{1}: (4, {})} | custom-call | flops 402653184 | bytes 1048576 | tf_op jit(solution)/shard_map/level_grads/pallas_call | solution.py:418
  21.0 0.5 %collective-permute-done.4.found_ref = f32[8,128,128]{2,1,0:T(8,128)S(1)} collective-permute-done((f32[8,128,128]{2,1,0:T(8,128)S(1)}, f32[8,128,128]{2,1,0:T(8,128)S(1)}, u32[]{:S(2)}, u32[]{:S(2)}) %collective-permute-start.4) | collective-permute-done | bytes 524320 | tf_op jit(solution)/shard_map/ppermute | solution.py:344
  21.5 0.1 pair.1
  21.6 0.4 collective-permute-start.8
  22.1 2.4 %collective-permute-start.5 = (f32[4,128,128]{2,1,0:T(8,128)S(1)}, f32[4,128,128]{2,1,0:T(8,128)S(1)}, u32[]{:S(2)}, u32[]{:S(2)}) collective-permute-start(f32[4,128,128]{2,1,0:T(8,128)S(1)} %get-tuple-element.63), channel_id=1, source_target_pairs={{0,24},{4,28},{8,16},{12,20},{16,8},{20,12},{24,0},{28,4},{1,25},{... | collective-permute-start | bytes 786440 | tf_op jit(solution)/shard_map/ppermute | solution.py:344
  24.5 0.5 %collective-permute-start.6 = (f32[4,128,128]{2,1,0:T(8,128)S(1)}, f32[4,128,128]{2,1,0:T(8,128)S(1)}, u32[]{:S(2)}, u32[]{:S(2)}) collective-permute-start(f32[4,128,128]{2,1,0:T(8,128)S(1)} %get-tuple-element.64), channel_id=1, source_target_pairs={{0,8},{4,12},{8,0},{12,4},{16,24},{20,28},{24,16},{28,20},{1,9},{5... | collective-permute-start | bytes 786440 | tf_op jit(solution)/shard_map/ppermute | solution.py:344
  25.1 0.5 %collective-permute-start.7 = (f32[4,128,128]{2,1,0:T(8,128)S(1)}, f32[4,128,128]{2,1,0:T(8,128)S(1)}, u32[]{:S(2)}, u32[]{:S(2)}) collective-permute-start(f32[4,128,128]{2,1,0:T(8,128)S(1)} %get-tuple-element.65), channel_id=1, source_target_pairs={{0,16},{4,20},{8,24},{12,28},{16,0},{20,4},{24,8},{28,12},{1,17},{... | collective-permute-start | bytes 786440 | tf_op jit(solution)/shard_map/ppermute | solution.py:344
  25.6 0.0 collective-permute-done.8.found_ref
  25.6 0.0 copy-done.2
  25.6 0.0 copy-done.4
  25.6 0.0 copy-done.6
  25.6 0.0 copy-done.8
  25.6 11.0 %local.1 = (bf16[4,8,256,128]{3,2,1,0:T(8,128)(2,1)S(1)}, bf16[4,8,256,128]{3,2,1,0:T(8,128)(2,1)S(1)}, bf16[4,8,256,128]{3,2,1,0:T(8,128)(2,1)S(1)}, f32[4,8,128,128]{3,2,1,0:T(8,128)S(1)}) custom-call(f32[14,1024]{1,0:T(8,128)S(1)} %fusion.lam_ref, bf16[4,8,256,128]{3,2,1,0:T(8,128)(2,1)S(1)} %copy-done.4, bf16[4,8,256,128]{3,2,1,0:T(8,128)(2,1)S(1)} %copy-done.6, ...), custom_call_target="tpu_custom_call" | custom-call | flops 3758096384 | bytes 4194304 | tf_op jit(solution)/shard_map/local/pallas_call | solution.py:448
  36.6 0.0 collective-permute-done.5.refs_0_
  36.6 0.4 %collective-permute-done.6.refs_1_ = f32[4,128,128]{2,1,0:T(8,128)S(1)} collective-permute-done((f32[4,128,128]{2,1,0:T(8,128)S(1)}, f32[4,128,128]{2,1,0:T(8,128)S(1)}, u32[]{:S(2)}, u32[]{:S(2)}) %collective-permute-start.6) | collective-permute-done | bytes 262176 | tf_op jit(solution)/shard_map/ppermute | solution.py:344
  37.0 0.0 collective-permute-done.7.refs_2_
  37.1 0.1 collective-permute-start.9
  37.2 1.3 %own_half.1 = (bf16[4,8,256,128]{3,2,1,0:T(8,128)(2,1)S(1)}, bf16[4,8,256,128]{3,2,1,0:T(8,128)(2,1)S(1)}, bf16[4,8,256,128]{3,2,1,0:T(8,128)(2,1)S(1)}) custom-call(f32[14,1024]{1,0:T(8,128)S(1)} %fusion.lam_ref, bf16[4,8,256,128]{3,2,1,0:T(8,128)(2,1)S(1)} %copy-done.4, ...), custom_call_target="tpu_custom_call", output_to_operand_aliasing={{0}: (6, {}), {1}: (7, {}), {2}: (8, {})} | custom-call | flops 671088640 | bytes 8388608 | tf_op jit(solution)/shard_map/own_half/pallas_call | solution.py:477
  38.5 0.6 %collective-permute-done.9.sums_ref = f32[2,4,128,128]{3,2,1,0:T(8,128)S(1)} collective-permute-done((f32[2,4,128,128]{3,2,1,0:T(8,128)S(1)}, f32[2,4,128,128]{3,2,1,0:T(8,128)S(1)}, u32[]{:S(2)}, u32[]{:S(2)}) %collective-permute-start.9) | collective-permute-done | bytes 524320 | tf_op jit(solution)/shard_map/ppermute | solution.py:344
  39.1 4.7 %final.1 = (bf16[1024,8,128]{2,1,0:T(8,128)(2,1)}, bf16[1024,8,128]{2,1,0:T(8,128)(2,1)}, bf16[1024,8,128]{2,1,0:T(8,128)(2,1)}) custom-call(f32[14,1024]{1,0:T(8,128)S(1)} %fusion.lam_ref, bf16[4,8,256,128]{3,2,1,0:T(8,128)(2,1)S(1)} %copy-done.4, bf16[4,8,256,128]{3,2,1,0:T(8,128)(2,1)S(1)} %copy-done.6, ...), custom_call_target="tpu_custom_call" | custom-call | flops 671088640 | bytes 16777216 | tf_op jit(solution)/shard_map/final/pallas_call | solution.py:489
  (4 shorter events, 0.1 us)
Async XLA Ops:
  0.6 16.1 %copy-start.9 = (s32[21,256]{1,0:T(8,128)S(1)}, s32[21,256]{1,0:T(8,128)}, u32[]{:S(2)}) copy-start(s32[21,256]{1,0:T(8,128)} %param.9) | copy-start | bytes 64516
  0.6 16.1 %collective-permute-start = (s32[21,256]{1,0:T(8,128)}, s32[21,256]{1,0:T(8,128)S(1)}, u32[]{:S(2)}, u32[]{:S(2)}) collective-permute-start(s32[21,256]{1,0:T(8,128)} %param.9), channel_id=1, source_target_pairs={{0,1},{1,2},{2,3},{3,0},{4,5},{5,6},{6,7},{7,4},{8,9},{9,10},{10,1... | collective-permute-start | bytes 64520 | tf_op jit(solution)/shard_map/ppermute | solution.py:396
  3.7 13.0 %collective-permute-start.2 = (s32[21,256]{1,0:T(8,128)}, s32[21,256]{1,0:T(8,128)S(1)}, u32[]{:S(2)}, u32[]{:S(2)}) collective-permute-start(s32[21,256]{1,0:T(8,128)} %param.9), channel_id=1, source_target_pairs={{0,3},{1,0},{2,1},{3,2},{4,7},{5,4},{6,5},{7,6},{8,11},{9,8},{10,9... | collective-permute-start | bytes 64520 | tf_op jit(solution)/shard_map/ppermute | solution.py:396
  5.8 10.9 %collective-permute-start.1 = (s32[21,256]{1,0:T(8,128)}, s32[21,256]{1,0:T(8,128)S(1)}, u32[]{:S(2)}, u32[]{:S(2)}) collective-permute-start(s32[21,256]{1,0:T(8,128)} %param.9), channel_id=1, source_target_pairs={{0,2},{1,3},{2,0},{3,1},{4,6},{5,7},{6,4},{7,5},{8,10},{9,11},{10,... | collective-permute-start | bytes 64520 | tf_op jit(solution)/shard_map/ppermute | solution.py:396
  11.7 1.3 %copy-start = (bf16[4,8,128,256]{3,2,1,0:T(8,128)(2,1)}, bf16[4,8,128,256]{3,2,1,0:T(8,128)(2,1)S(1)}, u32[]{:S(2)}) copy-start(bf16[4,8,128,256]{3,2,1,0:T(8,128)(2,1)S(1)} %get-tuple-element.52.qt_ref) | copy-start | bytes 6291460
  13.1 1.3 %copy-start.3 = (bf16[4,8,256,128]{3,2,1,0:T(8,128)(2,1)}, bf16[4,8,256,128]{3,2,1,0:T(8,128)(2,1)S(1)}, u32[]{:S(2)}) copy-start(bf16[4,8,256,128]{3,2,1,0:T(8,128)(2,1)S(1)} %get-tuple-element.48.k_ref) | copy-start | bytes 6291460
  14.4 1.3 %copy-start.5 = (bf16[4,8,256,128]{3,2,1,0:T(8,128)(2,1)}, bf16[4,8,256,128]{3,2,1,0:T(8,128)(2,1)S(1)}, u32[]{:S(2)}) copy-start(bf16[4,8,256,128]{3,2,1,0:T(8,128)(2,1)S(1)} %get-tuple-element.49.v_ref) | copy-start | bytes 6291460
  15.7 0.9 %copy-start.7 = (bf16[3,8,128,128]{3,2,1,0:T(8,128)(2,1)}, bf16[3,8,128,128]{3,2,1,0:T(8,128)(2,1)S(1)}, u32[]{:S(2)}) copy-start(bf16[3,8,128,128]{3,2,1,0:T(8,128)(2,1)S(1)} %get-tuple-element.66.level_ref) | copy-start | bytes 2359300
  16.6 2.8 %collective-permute-start.3 = (f32[4,128,128]{2,1,0:T(8,128)S(1)}, f32[4,128,128]{2,1,0:T(8,128)S(1)}, u32[]{:S(2)}, u32[]{:S(2)}) collective-permute-start(f32[4,128,128]{2,1,0:T(8,128)S(1)} %get-tuple-element.54), channel_id=1, source_target_pairs={{0,4},{4,0},{8,12},{12,8},{16,20},{20,16},{24,28},{28,24},{1,5},{5... | collective-permute-start | bytes 786440 | tf_op jit(solution)/shard_map/ppermute | solution.py:344
  16.9 1.6 %copy-start.1 = (bf16[4,8,128,256]{3,2,1,0:T(8,128)(2,1)S(1)}, bf16[4,8,128,256]{3,2,1,0:T(8,128)(2,1)}, u32[]{:S(2)}) copy-start(bf16[4,8,128,256]{3,2,1,0:T(8,128)(2,1)} %copy-done) | copy-start | bytes 6291460
  19.4 2.1 %collective-permute-start.4 = (f32[8,128,128]{2,1,0:T(8,128)S(1)}, f32[8,128,128]{2,1,0:T(8,128)S(1)}, u32[]{:S(2)}, u32[]{:S(2)}) collective-permute-start(f32[8,128,128]{2,1,0:T(8,128)S(1)} %get-tuple-element.58), channel_id=1, source_target_pairs={{0,4},{4,0},{8,12},{12,8},{16,20},{20,16},{24,28},{28,24},{1,5},{5... | collective-permute-start | bytes 1572872 | tf_op jit(solution)/shard_map/ppermute | solution.py:344
  20.0 5.6 %copy-start.2 = (bf16[4,8,128,256]{3,2,1,0:T(8,128)(2,1)S(1)}, bf16[4,8,128,256]{3,2,1,0:T(8,128)(2,1)}, u32[]{:S(2)}) copy-start(bf16[4,8,128,256]{3,2,1,0:T(8,128)(2,1)} %copy-done) | copy-start | bytes 6291460
  20.0 5.6 %copy-start.4 = (bf16[4,8,256,128]{3,2,1,0:T(8,128)(2,1)S(1)}, bf16[4,8,256,128]{3,2,1,0:T(8,128)(2,1)}, u32[]{:S(2)}) copy-start(bf16[4,8,256,128]{3,2,1,0:T(8,128)(2,1)} %copy-done.3) | copy-start | bytes 6291460
  20.0 5.6 %copy-start.6 = (bf16[4,8,256,128]{3,2,1,0:T(8,128)(2,1)S(1)}, bf16[4,8,256,128]{3,2,1,0:T(8,128)(2,1)}, u32[]{:S(2)}) copy-start(bf16[4,8,256,128]{3,2,1,0:T(8,128)(2,1)} %copy-done.5) | copy-start | bytes 6291460
  20.0 5.6 %copy-start.8 = (bf16[3,8,128,128]{3,2,1,0:T(8,128)(2,1)S(1)}, bf16[3,8,128,128]{3,2,1,0:T(8,128)(2,1)}, u32[]{:S(2)}) copy-start(bf16[3,8,128,128]{3,2,1,0:T(8,128)(2,1)} %copy-done.7) | copy-start | bytes 2359300
  21.6 3.9 %collective-permute-start.8 = (f32[8,128,128]{2,1,0:T(8,128)S(1)}, f32[8,128,128]{2,1,0:T(8,128)S(1)}, u32[]{:S(2)}, u32[]{:S(2)}) collective-permute-start(f32[8,128,128]{2,1,0:T(8,128)S(1)} %get-tuple-element.67), channel_id=1, source_target_pairs={{0,4},{4,0},{8,12},{12,8},{16,20},{20,16},{24,28},{28,24},{1,5},{5... | collective-permute-start | bytes 1572872 | tf_op jit(solution)/shard_map/ppermute | solution.py:344
  22.1 14.5 %collective-permute-start.5 = (f32[4,128,128]{2,1,0:T(8,128)S(1)}, f32[4,128,128]{2,1,0:T(8,128)S(1)}, u32[]{:S(2)}, u32[]{:S(2)}) collective-permute-start(f32[4,128,128]{2,1,0:T(8,128)S(1)} %get-tuple-element.63), channel_id=1, source_target_pairs={{0,24},{4,28},{8,16},{12,20},{16,8},{20,12},{24,0},{28,4},{1,25},{... | collective-permute-start | bytes 786440 | tf_op jit(solution)/shard_map/ppermute | solution.py:344
  24.5 12.5 %collective-permute-start.6 = (f32[4,128,128]{2,1,0:T(8,128)S(1)}, f32[4,128,128]{2,1,0:T(8,128)S(1)}, u32[]{:S(2)}, u32[]{:S(2)}) collective-permute-start(f32[4,128,128]{2,1,0:T(8,128)S(1)} %get-tuple-element.64), channel_id=1, source_target_pairs={{0,8},{4,12},{8,0},{12,4},{16,24},{20,28},{24,16},{28,20},{1,9},{5... | collective-permute-start | bytes 786440 | tf_op jit(solution)/shard_map/ppermute | solution.py:344
  25.1 12.0 %collective-permute-start.7 = (f32[4,128,128]{2,1,0:T(8,128)S(1)}, f32[4,128,128]{2,1,0:T(8,128)S(1)}, u32[]{:S(2)}, u32[]{:S(2)}) collective-permute-start(f32[4,128,128]{2,1,0:T(8,128)S(1)} %get-tuple-element.65), channel_id=1, source_target_pairs={{0,16},{4,20},{8,24},{12,28},{16,0},{20,4},{24,8},{28,12},{1,17},{... | collective-permute-start | bytes 786440 | tf_op jit(solution)/shard_map/ppermute | solution.py:344
  37.1 2.0 %collective-permute-start.9 = (f32[2,4,128,128]{3,2,1,0:T(8,128)S(1)}, f32[2,4,128,128]{3,2,1,0:T(8,128)S(1)}, u32[]{:S(2)}, u32[]{:S(2)}) collective-permute-start(f32[2,4,128,128]{3,2,1,0:T(8,128)S(1)} %sums.1.sums_ref), channel_id=1, source_target_pairs={{0,4},{4,0},{8,12},{12,8},{16,20},{20,16},{24,28},{28,24},{1,5},{5... | collective-permute-start | bytes 1572872 | tf_op jit(solution)/shard_map/ppermute | solution.py:344

commit v5 on v1

--- a/solution.py
+++ b/solution.py
@@ -72,38 +72,41 @@
                 level_ref[n, h] = state.astype(BF16)
 
 
-def grads_kernel(first_row, own, lam_ref, qt_ref, g_ref, state_ref, *refs):
-    sums_ref, whole_ref = refs[-2:]
+def grads_kernel(first_row, own, lam_ref, qt_ref, g_ref, state_ref, sums_ref, *whole_refs):
     chunks, heads, tile, width = g_ref.shape
     half = heads // 2
     levels = lam_ref.shape[0] - first_row
 
+    def level_grad(h, low, high):
+        weighted = [
+            stack_levels(
+                [
+                    scaled(
+                        lam_ref[first_row + b : first_row + b + 1, c * tile : (c + 1) * tile],
+                        qt_ref[c, h],
+                    )
+                    for b in range(low, high)
+                ],
+                0,
+            )
+            for c in range(chunks)
+        ]
+        grad = dot(stack_levels(weighted, 1), g_ref[:, h].reshape(chunks * tile, width))
+        return [grad[i * width : (i + 1) * width] for i in range(high - low)]
+
     for core in range(2):
 
         @pl.when(bit_of_block(0) == core)
         def _():
             for h in range(heads):
-                if (h // half == core) != own:
-                    continue
-                weighted = [
-                    stack_levels(
-                        [
-                            scaled(
-                                lam_ref[first_row + b : first_row + b + 1, c * tile : (c + 1) * tile],
-                                qt_ref[c, h],
-                            )
-                            for b in range(levels)
-                        ],
-                        0,
-                    )
-                    for c in range(chunks)
-                ]
-                grad = dot(stack_levels(weighted, 1), g_ref[:, h].reshape(chunks * tile, width))
-                parts = [grad[b * width : (b + 1) * width] for b in range(levels)]
-                state = state_ref[h]
-                whole_ref[h] = state if core == 0 else parts[0]
-                for b, part in enumerate([state, *parts[1:]]):
-                    sums_ref[b * half + h % half] = part
+                chosen = (h // half == core) == own
+                low = 0 if own and core == 1 else 1
+                parts = level_grad(h, low, levels if chosen else 1) if chosen or low == 0 else []
+                if own:
+                    whole_refs[0][h] = state_ref[h] if core == 0 else parts[0]
+                if chosen:
+                    for b, part in enumerate([state_ref[h], *parts[1 - low :]]):
+                        sums_ref[b * half + h % half] = part
 
 
 def make_mask(lam_ref, span, mask_ref):
@@ -400,22 +403,22 @@
 
     kh, vh, qt, gh, level_state, state = near(kh, vh, qt, gh, level_state, state)
 
-    def level_grads(own, before):
+    def level_grads(own):
         inputs = [lam, qt, gh, state]
+        sizes = (tree_bits * half, heads) if own else (tree_bits * half,)
         return pl.pallas_call(
             functools.partial(grads_kernel, local_bits + 1, own),
-            in_specs=[in_vmem] * len(inputs) + [anywhere] * len(before),
-            out_specs=[in_vmem] * 2,
-            out_shape=[pltpu.VMEM((n, *square), F32) for n in (tree_bits * half, heads)],
-            input_output_aliases={len(inputs): 1} if before else {},
+            in_specs=[in_vmem] * len(inputs),
+            out_specs=[in_vmem] * len(sizes),
+            out_shape=[pltpu.VMEM((n, *square), F32) for n in sizes],
             compiler_params=params(4),
             cost_estimate=cost(tree_bits * size * width, size),
             name="level_grads",
-        )(*inputs, *before)
-
-    send, everything = level_grads(False, [])
+        )(*inputs)
+
+    (send,) = level_grads(False)
     found = permute(send, 1)
-    keep, everything = level_grads(True, near(everything))
+    keep, everything = level_grads(True)
     (keep,) = near(keep)
     hops = [1 << b | m for b in range(1, tree_bits) for m in range(0, 1 << b, 2)]
     hops.sort(key=lambda hop: (hop & hop - 1) == 0)

time: 37.9 us -> 37.6 us (level)
  Pallas kernels: 24.2 us -> 23.6 us
    pallas_call x2, Pallas kernels: 1.99 us -> 1.46 us  [level_grads(): pl.pallas_call(functools.partial(grads_kernel, local_bits + 1, own), in_s...]
  transfers between devices with their start and end apart: 9 -> 9, of which waited for: 3 -> 3; matrix products, arithmetic and copies ran while one was open for 0% -> 0% of each run, Pallas kernels for 49% -> 48%
where the time goes in v5:
time: 37.6 us; the launch traced here: 37.5 us
  Pallas kernels  23.6 us (63%)
  starting transfers between devices  9.96 us (26%)
  waiting for transfers between devices  2.81 us (7%)
  between operations  0.95 us (3%)
    pallas_call x1, Pallas kernels, on_device(): pl.pallas_call(local_kernel, in_specs=[in_vmem] * 7, out_specs=[in_vmem]...  11 us
    ppermute x3, starting transfers between devices, on_device(): lax.ppermute(level_codes, 'head', [(i, (i + r) % groups) for i in range(g...  6.11 us
    pallas_call x1, Pallas kernels, on_device(): pl.pallas_call(functools.partial(states_kernel, pieces), grid=(chunks,),...  5 us
    pallas_call x1, Pallas kernels, on_device(): pl.pallas_call(functools.partial(final_kernel, local_bits + 2), in_specs=...  4.74 us
    ppermute x6, starting transfers between devices, permute(): return lax.ppermute(x, 'seq', [(i, i ^ apart) for i in range(blocks)])  3.85 us
    ppermute x6, waiting for transfers between devices, permute(): return lax.ppermute(x, 'seq', [(i, i ^ apart) for i in range(blocks)])  2.81 us
    pallas_call x2, Pallas kernels, level_grads(): pl.pallas_call(functools.partial(grads_kernel, local_bits + 1, own), in_s...  1.46 us
    pallas_call x1, Pallas kernels, on_device(): pl.pallas_call(functools.partial(own_half_kernel, local_bits + 2), in_spe...  1.34 us
  transfers between devices with their start and end apart: 9, of which 3 were waited for; matrix products, arithmetic and copies ran while one was open for 0% of the time, Pallas kernels for 48%

profile of v5, /device:TPU:0, one launch (start us, length us, event | category | flops | bytes accessed | tf_op | source)
XLA Modules:
  0.0 37.5 jit_solution(614923391182785602)
XLA Ops:
  0.6 3.1 %collective-permute-start = (s32[21,256]{1,0:T(8,128)}, s32[21,256]{1,0:T(8,128)S(1)}, u32[]{:S(2)}, u32[]{:S(2)}) collective-permute-start(s32[21,256]{1,0:T(8,128)} %param.9), channel_id=1, source_target_pairs={{0,1},{1,2},{2,3},{3,0},{4,5},{5,6},{6,7},{7,4},{8,9},{9,10},{10,1... | collective-permute-start | bytes 64520 | tf_op jit(solution)/shard_map/ppermute | solution.py:386
  3.7 2.1 %collective-permute-start.2 = (s32[21,256]{1,0:T(8,128)}, s32[21,256]{1,0:T(8,128)S(1)}, u32[]{:S(2)}, u32[]{:S(2)}) collective-permute-start(s32[21,256]{1,0:T(8,128)} %param.9), channel_id=1, source_target_pairs={{0,3},{1,0},{2,1},{3,2},{4,7},{5,4},{6,5},{7,6},{8,11},{9,8},{10,9... | collective-permute-start | bytes 64520 | tf_op jit(solution)/shard_map/ppermute | solution.py:386
  5.8 0.9 %collective-permute-start.1 = (s32[21,256]{1,0:T(8,128)}, s32[21,256]{1,0:T(8,128)S(1)}, u32[]{:S(2)}, u32[]{:S(2)}) collective-permute-start(s32[21,256]{1,0:T(8,128)} %param.9), channel_id=1, source_target_pairs={{0,2},{1,3},{2,0},{3,1},{4,6},{5,7},{6,4},{7,5},{8,10},{9,11},{10,... | collective-permute-start | bytes 64520 | tf_op jit(solution)/shard_map/ppermute | solution.py:386
  6.8 0.0 copy-start
  6.8 5.0 %states.1 = (bf16[4,8,256,128]{3,2,1,0:T(8,128)(2,1)S(1)}, bf16[4,8,256,128]{3,2,1,0:T(8,128)(2,1)S(1)}, bf16[4,8,256,128]{3,2,1,0:T(8,128)(2,1)S(1)}, bf16[4,8,...) custom-call(bf16[1024,8,128]{2,1,0:T(8,128)(2,1)} %refs_1_.1, ...), custom_call_target="tpu_custom_call" | custom-call | flops 268435456 | bytes 8388608 | tf_op jit(solution)/shard_map/states/pallas_call | solution.py:362
  11.8 0.0 collective-permute-done
  11.8 0.0 collective-permute-done.2
  11.8 0.0 collective-permute-done.1
  11.8 0.0 copy-done
  11.9 0.1 fusion.lam_ref
  12.0 0.7 %level_grads.3 = f32[12,128,128]{2,1,0:T(8,128)S(1)} custom-call(f32[14,1024]{1,0:T(8,128)S(1)} %fusion.lam_ref, bf16[4,8,128,256]{3,2,1,0:T(8,128)(2,1)S(1)} %get-tuple-element.46.qt_ref, bf16[4,8,256,128]{3,2,1,0:T(8,128)(2,1)S(1)} %get-tuple-element.45.g_ref, f32[8,128,128]{2,1,0:T(8,128)S(1)} %get-tuple-element.47.state_ref), custom_call_target="tpu_custom_call" | custom-call | flops 402653184 | bytes 1048576 | tf_op jit(solution)/shard_map/level_grads/pallas_call | solution.py:409
  12.7 0.1 collective-permute-start.3
  12.8 0.7 %level_grads.2 = (f32[12,128,128]{2,1,0:T(8,128)S(1)}, f32[8,128,128]{2,1,0:T(8,128)S(1)}) custom-call(f32[14,1024]{1,0:T(8,128)S(1)} %fusion.lam_ref, bf16[4,8,128,256]{3,2,1,0:T(8,128)(2,1)S(1)} %get-tuple-element.46.qt_ref, bf16[4,8,256,128]{3,2,1,0:T(8,128)(2,1)S(1)} %get-tuple-element.45.g_ref, f32[8,128,128]{2,1,0:T(8,128)S(1)} %get-tuple-element.47.state_ref), custom_call_target="tpu_custom_call" | custom-call | flops 402653184 | bytes 1048576 | tf_op jit(solution)/shard_map/level_grads/pallas_call | solution.py:409
  13.5 1.5 %collective-permute-done.3.found_ref = f32[12,128,128]{2,1,0:T(8,128)S(1)} collective-permute-done((f32[12,128,128]{2,1,0:T(8,128)S(1)}, f32[12,128,128]{2,1,0:T(8,128)S(1)}, u32[]{:S(2)}, u32[]{:S(2)}) %collective-permute-start.3) | collective-permute-done | bytes 786464 | tf_op jit(solution)/shard_map/ppermute | solution.py:337
  15.0 0.1 pair.1
  15.1 0.2 collective-permute-start.7
  15.3 2.5 %collective-permute-start.4 = (f32[4,128,128]{2,1,0:T(8,128)S(1)}, f32[4,128,128]{2,1,0:T(8,128)S(1)}, u32[]{:S(2)}, u32[]{:S(2)}) collective-permute-start(f32[4,128,128]{2,1,0:T(8,128)S(1)} %get-tuple-element.53), channel_id=1, source_target_pairs={{0,24},{4,28},{8,16},{12,20},{16,8},{20,12},{24,0},{28,4},{1,25},{... | collective-permute-start | bytes 786440 | tf_op jit(solution)/shard_map/ppermute | solution.py:337
  17.8 0.5 %collective-permute-start.5 = (f32[4,128,128]{2,1,0:T(8,128)S(1)}, f32[4,128,128]{2,1,0:T(8,128)S(1)}, u32[]{:S(2)}, u32[]{:S(2)}) collective-permute-start(f32[4,128,128]{2,1,0:T(8,128)S(1)} %get-tuple-element.54), channel_id=1, source_target_pairs={{0,8},{4,12},{8,0},{12,4},{16,24},{20,28},{24,16},{28,20},{1,9},{5... | collective-permute-start | bytes 786440 | tf_op jit(solution)/shard_map/ppermute | solution.py:337
  18.3 0.5 %collective-permute-start.6 = (f32[4,128,128]{2,1,0:T(8,128)S(1)}, f32[4,128,128]{2,1,0:T(8,128)S(1)}, u32[]{:S(2)}, u32[]{:S(2)}) collective-permute-start(f32[4,128,128]{2,1,0:T(8,128)S(1)} %get-tuple-element.55), channel_id=1, source_target_pairs={{0,16},{4,20},{8,24},{12,28},{16,0},{20,4},{24,8},{28,12},{1,17},{... | collective-permute-start | bytes 786440 | tf_op jit(solution)/shard_map/ppermute | solution.py:337
  18.9 0.0 collective-permute-done.7.found_ref
  18.9 11.0 %local.1 = (bf16[4,8,256,128]{3,2,1,0:T(8,128)(2,1)S(1)}, bf16[4,8,256,128]{3,2,1,0:T(8,128)(2,1)S(1)}, bf16[4,8,256,128]{3,2,1,0:T(8,128)(2,1)S(1)}, f32[4,8,128,128]{3,2,1,0:T(8,128)S(1)}) custom-call(f32[14,1024]{1,0:T(8,128)S(1)} %fusion.lam_ref, bf16[4,8,256,128]{3,2,1,0:T(8,128)(2,1)S(1)} %get-tuple-element.43.k_ref, ...), custom_call_target="tpu_custom_call" | custom-call | flops 3758096384 | bytes 4194304 | tf_op jit(solution)/shard_map/local/pallas_call | solution.py:437
  29.8 0.0 collective-permute-done.4.refs_0_
  29.8 0.7 %collective-permute-done.5.refs_1_ = f32[4,128,128]{2,1,0:T(8,128)S(1)} collective-permute-done((f32[4,128,128]{2,1,0:T(8,128)S(1)}, f32[4,128,128]{2,1,0:T(8,128)S(1)}, u32[]{:S(2)}, u32[]{:S(2)}) %collective-permute-start.5) | collective-permute-done | bytes 262176 | tf_op jit(solution)/shard_map/ppermute | solution.py:337
  30.5 0.0 collective-permute-done.6.refs_2_
  30.6 0.1 collective-permute-start.8
  30.7 1.3 %own_half.1 = (bf16[4,8,256,128]{3,2,1,0:T(8,128)(2,1)S(1)}, bf16[4,8,256,128]{3,2,1,0:T(8,128)(2,1)S(1)}, bf16[4,8,256,128]{3,2,1,0:T(8,128)(2,1)S(1)}) custom-call(f32[14,1024]{1,0:T(8,128)S(1)} %fusion.lam_ref, bf16[4,8,256,128]{3,2,1,0:T(8,128)(2,1)S(1)} %get-tuple-element.43.k_ref, ...), custom_call_target="tpu_custom_call", output_to_operand_aliasing={{0}: (6, {}), {1}: (7, {}), {2}: (8, {})} | custom-call | flops 671088640 | bytes 8388608 | tf_op jit(solution)/shard_map/own_half/pallas_call | solution.py:466
  32.0 0.6 %collective-permute-done.8.sums_ref = f32[2,4,128,128]{3,2,1,0:T(8,128)S(1)} collective-permute-done((f32[2,4,128,128]{3,2,1,0:T(8,128)S(1)}, f32[2,4,128,128]{3,2,1,0:T(8,128)S(1)}, u32[]{:S(2)}, u32[]{:S(2)}) %collective-permute-start.8) | collective-permute-done | bytes 524320 | tf_op jit(solution)/shard_map/ppermute | solution.py:337
  32.6 4.7 %final.1 = (bf16[1024,8,128]{2,1,0:T(8,128)(2,1)}, bf16[1024,8,128]{2,1,0:T(8,128)(2,1)}, bf16[1024,8,128]{2,1,0:T(8,128)(2,1)}) custom-call(f32[14,1024]{1,0:T(8,128)S(1)} %fusion.lam_ref, bf16[4,8,256,128]{3,2,1,0:T(8,128)(2,1)S(1)} %get-tuple-element.43.k_ref, bf16[4,8,256,128]{3,2,1,0:T(8,128)(2,1)S(1)} %get-tuple-element.44.v_ref, ...), custom_call_target="tpu_custom_call" | custom-call | flops 671088640 | bytes 16777216 | tf_op jit(solution)/shard_map/final/pallas_call | solution.py:478
  (4 shorter events, 0.1 us)
Async XLA Ops:
  0.6 11.2 %collective-permute-start = (s32[21,256]{1,0:T(8,128)}, s32[21,256]{1,0:T(8,128)S(1)}, u32[]{:S(2)}, u32[]{:S(2)}) collective-permute-start(s32[21,256]{1,0:T(8,128)} %param.9), channel_id=1, source_target_pairs={{0,1},{1,2},{2,3},{3,0},{4,5},{5,6},{6,7},{7,4},{8,9},{9,10},{10,1... | collective-permute-start | bytes 64520 | tf_op jit(solution)/shard_map/ppermute | solution.py:386
  3.7 8.1 %collective-permute-start.2 = (s32[21,256]{1,0:T(8,128)}, s32[21,256]{1,0:T(8,128)S(1)}, u32[]{:S(2)}, u32[]{:S(2)}) collective-permute-start(s32[21,256]{1,0:T(8,128)} %param.9), channel_id=1, source_target_pairs={{0,3},{1,0},{2,1},{3,2},{4,7},{5,4},{6,5},{7,6},{8,11},{9,8},{10,9... | collective-permute-start | bytes 64520 | tf_op jit(solution)/shard_map/ppermute | solution.py:386
  5.8 6.0 %collective-permute-start.1 = (s32[21,256]{1,0:T(8,128)}, s32[21,256]{1,0:T(8,128)S(1)}, u32[]{:S(2)}, u32[]{:S(2)}) collective-permute-start(s32[21,256]{1,0:T(8,128)} %param.9), channel_id=1, source_target_pairs={{0,2},{1,3},{2,0},{3,1},{4,6},{5,7},{6,4},{7,5},{8,10},{9,11},{10,... | collective-permute-start | bytes 64520 | tf_op jit(solution)/shard_map/ppermute | solution.py:386
  6.8 5.1 %copy-start = (s32[21,256]{1,0:T(8,128)S(1)}, s32[21,256]{1,0:T(8,128)}, u32[]{:S(2)}) copy-start(s32[21,256]{1,0:T(8,128)} %param.9) | copy-start | bytes 64516
  12.7 2.4 %collective-permute-start.3 = (f32[12,128,128]{2,1,0:T(8,128)S(1)}, f32[12,128,128]{2,1,0:T(8,128)S(1)}, u32[]{:S(2)}, u32[]{:S(2)}) collective-permute-start(f32[12,128,128]{2,1,0:T(8,128)S(1)} %level_grads.3), channel_id=1, source_target_pairs={{0,4},{4,0},{8,12},{12,8},{16,20},{20,16},{24,28},{28,24},{1,5},{5... | collective-permute-start | bytes 2359304 | tf_op jit(solution)/shard_map/ppermute | solution.py:337
  15.1 3.7 %collective-permute-start.7 = (f32[8,128,128]{2,1,0:T(8,128)S(1)}, f32[8,128,128]{2,1,0:T(8,128)S(1)}, u32[]{:S(2)}, u32[]{:S(2)}) collective-permute-start(f32[8,128,128]{2,1,0:T(8,128)S(1)} %get-tuple-element.57), channel_id=1, source_target_pairs={{0,4},{4,0},{8,12},{12,8},{16,20},{20,16},{24,28},{28,24},{1,5},{5... | collective-permute-start | bytes 1572872 | tf_op jit(solution)/shard_map/ppermute | solution.py:337
  15.3 14.5 %collective-permute-start.4 = (f32[4,128,128]{2,1,0:T(8,128)S(1)}, f32[4,128,128]{2,1,0:T(8,128)S(1)}, u32[]{:S(2)}, u32[]{:S(2)}) collective-permute-start(f32[4,128,128]{2,1,0:T(8,128)S(1)} %get-tuple-element.53), channel_id=1, source_target_pairs={{0,24},{4,28},{8,16},{12,20},{16,8},{20,12},{24,0},{28,4},{1,25},{... | collective-permute-start | bytes 786440 | tf_op jit(solution)/shard_map/ppermute | solution.py:337
  17.8 12.7 %collective-permute-start.5 = (f32[4,128,128]{2,1,0:T(8,128)S(1)}, f32[4,128,128]{2,1,0:T(8,128)S(1)}, u32[]{:S(2)}, u32[]{:S(2)}) collective-permute-start(f32[4,128,128]{2,1,0:T(8,128)S(1)} %get-tuple-element.54), channel_id=1, source_target_pairs={{0,8},{4,12},{8,0},{12,4},{16,24},{20,28},{24,16},{28,20},{1,9},{5... | collective-permute-start | bytes 786440 | tf_op jit(solution)/shard_map/ppermute | solution.py:337
  18.3 12.2 %collective-permute-start.6 = (f32[4,128,128]{2,1,0:T(8,128)S(1)}, f32[4,128,128]{2,1,0:T(8,128)S(1)}, u32[]{:S(2)}, u32[]{:S(2)}) collective-permute-start(f32[4,128,128]{2,1,0:T(8,128)S(1)} %get-tuple-element.55), channel_id=1, source_target_pairs={{0,16},{4,20},{8,24},{12,28},{16,0},{20,4},{24,8},{28,12},{1,17},{... | collective-permute-start | bytes 786440 | tf_op jit(solution)/shard_map/ppermute | solution.py:337
  30.6 2.0 %collective-permute-start.8 = (f32[2,4,128,128]{3,2,1,0:T(8,128)S(1)}, f32[2,4,128,128]{3,2,1,0:T(8,128)S(1)}, u32[]{:S(2)}, u32[]{:S(2)}) collective-permute-start(f32[2,4,128,128]{3,2,1,0:T(8,128)S(1)} %sums.1.sums_ref), channel_id=1, source_target_pairs={{0,4},{4,0},{8,12},{12,8},{16,20},{20,16},{24,28},{28,24},{1,5},{5... | collective-permute-start | bytes 1572872 | tf_op jit(solution)/shard_map/ppermute | solution.py:337

commit v6 on v5

--- a/solution.py
+++ b/solution.py
@@ -247,18 +247,18 @@
     for i in range(half):
         half_ref[i], state_ref[i] = received(sums_ref, i)
     for c in range(chunks):
-        widen(lam_ref, first_row, slice(c * tile, (c + 1) * tile), wide_ref)
+        widen(lam_ref, first_row, slice(c * tile, (c + 1) * tile), wide_ref.at[c])
         for i in range(half):
             h = start + i
-            dq_ref[c, h] = add_to_query(half_ref[i], wide_ref, g_ref[c, h], dq_in[c, h])
+            dq_ref[c, h] = add_to_query(half_ref[i], wide_ref.at[c], g_ref[c, h], dq_in[c, h])
             dk_ref[c, h], dv_ref[c, h] = add_to_key_value(
                 gin_ref[c, h] + state_ref[i], k_ref[c, h], v_ref[c, h], dk_in[c, h], dv_in[c, h]
             )
 
 
 def final_kernel(
-    first_row, lam_ref, k_ref, v_ref, g_ref, dq_in, dk_in, dv_in, gin_ref, sums_ref,
-    dq_out, dk_out, dv_out, done_ref, wide_ref, half_ref, state_ref, sems,
+    wide_ref, k_ref, v_ref, g_ref, dq_in, dk_in, dv_in, gin_ref, sums_ref,
+    dq_out, dk_out, dv_out, done_ref, half_ref, state_ref, sems,
 ):
     chunks, heads, tile, _ = k_ref.shape
     half = half_ref.shape[0]
@@ -284,13 +284,12 @@
         @pl.when(bit_of_block(0) == core)
         def _():
             for c in range(chunks):
-                widen(lam_ref, first_row, slice(c * tile, (c + 1) * tile), wide_ref)
                 queries, keys, values = [], [], []
                 for h in range(heads):
                     query, key, value = dq_in[c, h], dk_in[c, h], dv_in[c, h]
                     if h // half != core:
                         i = h % half
-                        query = add_to_query(half_ref[i], wide_ref, g_ref[c, h], query)
+                        query = add_to_query(half_ref[i], wide_ref.at[c], g_ref[c, h], query)
                         key, value = add_to_key_value(
                             gin_ref[c, h] + state_ref[i], k_ref[c, h], v_ref[c, h], key, value
                         )
@@ -458,16 +457,15 @@
     others = permute(mine, 1)
 
     kept = [
-        pltpu.VMEM((tree_bits - 1, tile, width), F32),
         pltpu.VMEM((half, (tree_bits - 1) * width, width), BF16),
         pltpu.VMEM((half, *square), F32),
     ]
     gin, mine = near(gin, mine)
-    parts = pl.pallas_call(
+    *parts, wide = pl.pallas_call(
         functools.partial(own_half_kernel, local_bits + 2),
         in_specs=[in_vmem] * 9,
-        out_specs=[in_vmem] * 3,
-        out_shape=[natural] * 3,
+        out_specs=[in_vmem] * 4,
+        out_shape=[natural] * 3 + [pltpu.VMEM((chunks, tree_bits - 1, tile, width), F32)],
         input_output_aliases={6: 0, 7: 1, 8: 2},
         scratch_shapes=kept,
         compiler_params=params(3),
@@ -476,7 +474,7 @@
     )(lam, kh, vh, gh, gin, mine, *near(*parts))
     others, parts = lax.optimization_barrier((others, parts))
     return pl.pallas_call(
-        functools.partial(final_kernel, local_bits + 2),
+        final_kernel,
         in_specs=[in_vmem] * 9,
         out_specs=[anywhere] * 3,
         out_shape=[pltpu.HBM((count, heads, width), BF16)] * 3,
@@ -487,7 +485,7 @@
         compiler_params=params(10),
         cost_estimate=cost((tree_bits + 2) * size * width, 16 * size),
         name="final",
-    )(lam, kh, vh, gh, *near(*parts), gin, others)
+    )(*near(wide), kh, vh, gh, *near(*parts), gin, others)
 
 
 def solution(mesh):

time: 37.6 us -> 38.7 us (1.029)
  starting transfers between devices: 9.96 us -> 10.9 us
    ppermute x3, starting transfers between devices: 6.11 us -> 7.01 us  [on_device(): lax.ppermute(level_codes, 'head', [(i, (i + r) % groups) for i in range(g...]
  transfers between devices with their start and end apart: 9 -> 9, of which waited for: 3 -> 3; matrix products, arithmetic and copies ran while one was open for 0% -> 0% of each run, Pallas kernels for 48% -> 47%
where the time goes in v6:
time: 38.7 us; the launch traced here: 38.5 us
  Pallas kernels  23.9 us (62%)
  starting transfers between devices  10.9 us (28%)
  waiting for transfers between devices  2.68 us (7%)
  between operations  0.95 us (2%)
    pallas_call x1, Pallas kernels, on_device(): pl.pallas_call(local_kernel, in_specs=[in_vmem] * 7, out_specs=[in_vmem]...  11 us
    ppermute x3, starting transfers between devices, on_device(): lax.ppermute(level_codes, 'head', [(i, (i + r) % groups) for i in range(g...  7.01 us
    pallas_call x1, Pallas kernels, on_device(): pl.pallas_call(functools.partial(states_kernel, pieces), grid=(chunks,),...  5 us
    pallas_call x1, Pallas kernels, on_device(): pl.pallas_call(final_kernel, in_specs=[in_vmem] * 9, out_specs=[anywhere]...  4.88 us
    ppermute x6, starting transfers between devices, permute(): return lax.ppermute(x, 'seq', [(i, i ^ apart) for i in range(blocks)])  3.85 us
    ppermute x6, waiting for transfers between devices, permute(): return lax.ppermute(x, 'seq', [(i, i ^ apart) for i in range(blocks)])  2.67 us
    pallas_call x2, Pallas kernels, level_grads(): pl.pallas_call(functools.partial(grads_kernel, local_bits + 1, own), in_s...  1.47 us
    pallas_call x1, Pallas kernels, on_device(): pl.pallas_call(functools.partial(own_half_kernel, local_bits + 2), in_spe...  1.45 us
  transfers between devices with their start and end apart: 9, of which 3 were waited for; matrix products, arithmetic and copies ran while one was open for 0% of the time, Pallas kernels for 47%

profile of v6, /device:TPU:0, one launch (start us, length us, event | category | flops | bytes accessed | tf_op | source)
XLA Modules:
  0.0 38.5 jit_solution(8419503105718634162)
XLA Ops:
  0.6 3.1 %collective-permute-start = (s32[21,256]{1,0:T(8,128)}, s32[21,256]{1,0:T(8,128)S(1)}, u32[]{:S(2)}, u32[]{:S(2)}) collective-permute-start(s32[21,256]{1,0:T(8,128)} %param.9), channel_id=1, source_target_pairs={{0,1},{1,2},{2,3},{3,0},{4,5},{5,6},{6,7},{7,4},{8,9},{9,10},{10,1... | collective-permute-start | bytes 64520 | tf_op jit(solution)/shard_map/ppermute | solution.py:385
  3.7 2.6 %collective-permute-start.1 = (s32[21,256]{1,0:T(8,128)}, s32[21,256]{1,0:T(8,128)S(1)}, u32[]{:S(2)}, u32[]{:S(2)}) collective-permute-start(s32[21,256]{1,0:T(8,128)} %param.9), channel_id=1, source_target_pairs={{0,2},{1,3},{2,0},{3,1},{4,6},{5,7},{6,4},{7,5},{8,10},{9,11},{10,... | collective-permute-start | bytes 64520 | tf_op jit(solution)/shard_map/ppermute | solution.py:385
  6.3 1.3 %collective-permute-start.2 = (s32[21,256]{1,0:T(8,128)}, s32[21,256]{1,0:T(8,128)S(1)}, u32[]{:S(2)}, u32[]{:S(2)}) collective-permute-start(s32[21,256]{1,0:T(8,128)} %param.9), channel_id=1, source_target_pairs={{0,3},{1,0},{2,1},{3,2},{4,7},{5,4},{6,5},{7,6},{8,11},{9,8},{10,9... | collective-permute-start | bytes 64520 | tf_op jit(solution)/shard_map/ppermute | solution.py:385
  7.7 0.0 copy-start
  7.7 5.0 %states.1 = (bf16[4,8,256,128]{3,2,1,0:T(8,128)(2,1)S(1)}, bf16[4,8,256,128]{3,2,1,0:T(8,128)(2,1)S(1)}, bf16[4,8,256,128]{3,2,1,0:T(8,128)(2,1)S(1)}, bf16[4,8,...) custom-call(bf16[1024,8,128]{2,1,0:T(8,128)(2,1)} %refs_1_.1, ...), custom_call_target="tpu_custom_call" | custom-call | flops 268435456 | bytes 8388608 | tf_op jit(solution)/shard_map/states/pallas_call | solution.py:361
  12.7 0.0 collective-permute-done
  12.7 0.0 collective-permute-done.1
  12.7 0.0 collective-permute-done.2
  12.7 0.0 copy-done
  12.8 0.1 fusion.lam_ref
  12.9 0.7 %level_grads.3 = f32[12,128,128]{2,1,0:T(8,128)S(1)} custom-call(f32[14,1024]{1,0:T(8,128)S(1)} %fusion.lam_ref, bf16[4,8,128,256]{3,2,1,0:T(8,128)(2,1)S(1)} %get-tuple-element.47.qt_ref, bf16[4,8,256,128]{3,2,1,0:T(8,128)(2,1)S(1)} %get-tuple-element.46.g_ref, f32[8,128,128]{2,1,0:T(8,128)S(1)} %get-tuple-element.49.state_ref), custom_call_target="tpu_custom_call" | custom-call | flops 402653184 | bytes 1048576 | tf_op jit(solution)/shard_map/level_grads/pallas_call | solution.py:408
  13.6 0.1 collective-permute-start.3
  13.7 0.7 %level_grads.2 = (f32[12,128,128]{2,1,0:T(8,128)S(1)}, f32[8,128,128]{2,1,0:T(8,128)S(1)}) custom-call(f32[14,1024]{1,0:T(8,128)S(1)} %fusion.lam_ref, bf16[4,8,128,256]{3,2,1,0:T(8,128)(2,1)S(1)} %get-tuple-element.47.qt_ref, bf16[4,8,256,128]{3,2,1,0:T(8,128)(2,1)S(1)} %get-tuple-element.46.g_ref, f32[8,128,128]{2,1,0:T(8,128)S(1)} %get-tuple-element.49.state_ref), custom_call_target="tpu_custom_call" | custom-call | flops 402653184 | bytes 1048576 | tf_op jit(solution)/shard_map/level_grads/pallas_call | solution.py:408
  14.4 1.5 %collective-permute-done.3.found_ref = f32[12,128,128]{2,1,0:T(8,128)S(1)} collective-permute-done((f32[12,128,128]{2,1,0:T(8,128)S(1)}, f32[12,128,128]{2,1,0:T(8,128)S(1)}, u32[]{:S(2)}, u32[]{:S(2)}) %collective-permute-start.3) | collective-permute-done | bytes 786464 | tf_op jit(solution)/shard_map/ppermute | solution.py:336
  15.9 0.1 pair.1
  16.1 0.2 collective-permute-start.4
  16.3 2.5 %collective-permute-start.5 = (f32[4,128,128]{2,1,0:T(8,128)S(1)}, f32[4,128,128]{2,1,0:T(8,128)S(1)}, u32[]{:S(2)}, u32[]{:S(2)}) collective-permute-start(f32[4,128,128]{2,1,0:T(8,128)S(1)} %get-tuple-element.57), channel_id=1, source_target_pairs={{0,24},{4,28},{8,16},{12,20},{16,8},{20,12},{24,0},{28,4},{1,25},{... | collective-permute-start | bytes 786440 | tf_op jit(solution)/shard_map/ppermute | solution.py:336
  18.7 0.5 %collective-permute-start.6 = (f32[4,128,128]{2,1,0:T(8,128)S(1)}, f32[4,128,128]{2,1,0:T(8,128)S(1)}, u32[]{:S(2)}, u32[]{:S(2)}) collective-permute-start(f32[4,128,128]{2,1,0:T(8,128)S(1)} %get-tuple-element.58), channel_id=1, source_target_pairs={{0,8},{4,12},{8,0},{12,4},{16,24},{20,28},{24,16},{28,20},{1,9},{5... | collective-permute-start | bytes 786440 | tf_op jit(solution)/shard_map/ppermute | solution.py:336
  19.2 0.5 %collective-permute-start.7 = (f32[4,128,128]{2,1,0:T(8,128)S(1)}, f32[4,128,128]{2,1,0:T(8,128)S(1)}, u32[]{:S(2)}, u32[]{:S(2)}) collective-permute-start(f32[4,128,128]{2,1,0:T(8,128)S(1)} %get-tuple-element.59), channel_id=1, source_target_pairs={{0,16},{4,20},{8,24},{12,28},{16,0},{20,4},{24,8},{28,12},{1,17},{... | collective-permute-start | bytes 786440 | tf_op jit(solution)/shard_map/ppermute | solution.py:336
  19.8 0.0 collective-permute-done.4.found_ref
  19.8 11.0 %local.1 = (bf16[4,8,256,128]{3,2,1,0:T(8,128)(2,1)S(1)}, bf16[4,8,256,128]{3,2,1,0:T(8,128)(2,1)S(1)}, bf16[4,8,256,128]{3,2,1,0:T(8,128)(2,1)S(1)}, f32[4,8,128,128]{3,2,1,0:T(8,128)S(1)}) custom-call(f32[14,1024]{1,0:T(8,128)S(1)} %fusion.lam_ref, bf16[4,8,256,128]{3,2,1,0:T(8,128)(2,1)S(1)} %get-tuple-element.44.k_ref, ...), custom_call_target="tpu_custom_call" | custom-call | flops 3758096384 | bytes 4194304 | tf_op jit(solution)/shard_map/local/pallas_call | solution.py:436
  30.7 0.0 collective-permute-done.5.refs_0_
  30.8 0.7 %collective-permute-done.6.refs_1_ = f32[4,128,128]{2,1,0:T(8,128)S(1)} collective-permute-done((f32[4,128,128]{2,1,0:T(8,128)S(1)}, f32[4,128,128]{2,1,0:T(8,128)S(1)}, u32[]{:S(2)}, u32[]{:S(2)}) %collective-permute-start.6) | collective-permute-done | bytes 262176 | tf_op jit(solution)/shard_map/ppermute | solution.py:336
  31.4 0.0 collective-permute-done.7.refs_2_
  31.5 0.1 collective-permute-start.8
  31.6 1.4 %own_half.1 = (bf16[4,8,256,128]{3,2,1,0:T(8,128)(2,1)S(1)}, bf16[4,8,256,128]{3,2,1,0:T(8,128)(2,1)S(1)}, bf16[4,8,256,128]{3,2,1,0:T(8,128)(2,1)S(1)}, f32[4,2,256,128]{3,2,1,0:T(8,128)S(1)}) custom-call(f32[14,1024]{1,0:T(8,128)S(1)} %fusion.lam_ref, ...), custom_call_target="tpu_custom_call", output_to_operand_aliasing={{0}: (6, {}), {1}: (7, {}), {2}: (8, {})} | custom-call | flops 671088640 | bytes 8388608 | tf_op jit(solution)/shard_map/own_half/pallas_call | solution.py:464
  33.0 0.4 %collective-permute-done.8.sums_ref = f32[2,4,128,128]{3,2,1,0:T(8,128)S(1)} collective-permute-done((f32[2,4,128,128]{3,2,1,0:T(8,128)S(1)}, f32[2,4,128,128]{3,2,1,0:T(8,128)S(1)}, u32[]{:S(2)}, u32[]{:S(2)}) %collective-permute-start.8) | collective-permute-done | bytes 524320 | tf_op jit(solution)/shard_map/ppermute | solution.py:336
  33.5 4.9 %final.1 = (bf16[1024,8,128]{2,1,0:T(8,128)(2,1)}, bf16[1024,8,128]{2,1,0:T(8,128)(2,1)}, bf16[1024,8,128]{2,1,0:T(8,128)(2,1)}) custom-call(f32[4,2,256,128]{3,2,1,0:T(8,128)S(1)} %get-tuple-element.69.wide_ref, bf16[4,8,256,128]{3,2,1,0:T(8,128)(2,1)S(1)} %get-tuple-element.44.k_ref, bf16[4,8,256,128]{3,2,1,0:T(8,128)(2,1)S(1)} %get-tuple-element.45.v_ref, ...), custom_call_target="tpu_custom_call" | custom-call | flops 671088640 | bytes 16777216 | tf_op jit(solution)/shard_map/final/pallas_call | solution.py:476
  (4 shorter events, 0.1 us)
Async XLA Ops:
  0.6 12.1 %collective-permute-start = (s32[21,256]{1,0:T(8,128)}, s32[21,256]{1,0:T(8,128)S(1)}, u32[]{:S(2)}, u32[]{:S(2)}) collective-permute-start(s32[21,256]{1,0:T(8,128)} %param.9), channel_id=1, source_target_pairs={{0,1},{1,2},{2,3},{3,0},{4,5},{5,6},{6,7},{7,4},{8,9},{9,10},{10,1... | collective-permute-start | bytes 64520 | tf_op jit(solution)/shard_map/ppermute | solution.py:385
  3.7 9.0 %collective-permute-start.1 = (s32[21,256]{1,0:T(8,128)}, s32[21,256]{1,0:T(8,128)S(1)}, u32[]{:S(2)}, u32[]{:S(2)}) collective-permute-start(s32[21,256]{1,0:T(8,128)} %param.9), channel_id=1, source_target_pairs={{0,2},{1,3},{2,0},{3,1},{4,6},{5,7},{6,4},{7,5},{8,10},{9,11},{10,... | collective-permute-start | bytes 64520 | tf_op jit(solution)/shard_map/ppermute | solution.py:385
  6.3 6.4 %collective-permute-start.2 = (s32[21,256]{1,0:T(8,128)}, s32[21,256]{1,0:T(8,128)S(1)}, u32[]{:S(2)}, u32[]{:S(2)}) collective-permute-start(s32[21,256]{1,0:T(8,128)} %param.9), channel_id=1, source_target_pairs={{0,3},{1,0},{2,1},{3,2},{4,7},{5,4},{6,5},{7,6},{8,11},{9,8},{10,9... | collective-permute-start | bytes 64520 | tf_op jit(solution)/shard_map/ppermute | solution.py:385
  7.7 5.1 %copy-start = (s32[21,256]{1,0:T(8,128)S(1)}, s32[21,256]{1,0:T(8,128)}, u32[]{:S(2)}) copy-start(s32[21,256]{1,0:T(8,128)} %param.9) | copy-start | bytes 64516
  13.6 2.4 %collective-permute-start.3 = (f32[12,128,128]{2,1,0:T(8,128)S(1)}, f32[12,128,128]{2,1,0:T(8,128)S(1)}, u32[]{:S(2)}, u32[]{:S(2)}) collective-permute-start(f32[12,128,128]{2,1,0:T(8,128)S(1)} %level_grads.3), channel_id=1, source_target_pairs={{0,4},{4,0},{8,12},{12,8},{16,20},{20,16},{24,28},{28,24},{1,5},{5... | collective-permute-start | bytes 2359304 | tf_op jit(solution)/shard_map/ppermute | solution.py:336
  16.1 3.7 %collective-permute-start.4 = (f32[8,128,128]{2,1,0:T(8,128)S(1)}, f32[8,128,128]{2,1,0:T(8,128)S(1)}, u32[]{:S(2)}, u32[]{:S(2)}) collective-permute-start(f32[8,128,128]{2,1,0:T(8,128)S(1)} %get-tuple-element.55), channel_id=1, source_target_pairs={{0,4},{4,0},{8,12},{12,8},{16,20},{20,16},{24,28},{28,24},{1,5},{5... | collective-permute-start | bytes 1572872 | tf_op jit(solution)/shard_map/ppermute | solution.py:336
  16.3 14.5 %collective-permute-start.5 = (f32[4,128,128]{2,1,0:T(8,128)S(1)}, f32[4,128,128]{2,1,0:T(8,128)S(1)}, u32[]{:S(2)}, u32[]{:S(2)}) collective-permute-start(f32[4,128,128]{2,1,0:T(8,128)S(1)} %get-tuple-element.57), channel_id=1, source_target_pairs={{0,24},{4,28},{8,16},{12,20},{16,8},{20,12},{24,0},{28,4},{1,25},{... | collective-permute-start | bytes 786440 | tf_op jit(solution)/shard_map/ppermute | solution.py:336
  18.7 12.7 %collective-permute-start.6 = (f32[4,128,128]{2,1,0:T(8,128)S(1)}, f32[4,128,128]{2,1,0:T(8,128)S(1)}, u32[]{:S(2)}, u32[]{:S(2)}) collective-permute-start(f32[4,128,128]{2,1,0:T(8,128)S(1)} %get-tuple-element.58), channel_id=1, source_target_pairs={{0,8},{4,12},{8,0},{12,4},{16,24},{20,28},{24,16},{28,20},{1,9},{5... | collective-permute-start | bytes 786440 | tf_op jit(solution)/shard_map/ppermute | solution.py:336
  19.2 12.2 %collective-permute-start.7 = (f32[4,128,128]{2,1,0:T(8,128)S(1)}, f32[4,128,128]{2,1,0:T(8,128)S(1)}, u32[]{:S(2)}, u32[]{:S(2)}) collective-permute-start(f32[4,128,128]{2,1,0:T(8,128)S(1)} %get-tuple-element.59), channel_id=1, source_target_pairs={{0,16},{4,20},{8,24},{12,28},{16,0},{20,4},{24,8},{28,12},{1,17},{... | collective-permute-start | bytes 786440 | tf_op jit(solution)/shard_map/ppermute | solution.py:336
  31.5 2.0 %collective-permute-start.8 = (f32[2,4,128,128]{3,2,1,0:T(8,128)S(1)}, f32[2,4,128,128]{3,2,1,0:T(8,128)S(1)}, u32[]{:S(2)}, u32[]{:S(2)}) collective-permute-start(f32[2,4,128,128]{3,2,1,0:T(8,128)S(1)} %sums.1.sums_ref), channel_id=1, source_target_pairs={{0,4},{4,0},{8,12},{12,8},{16,20},{20,16},{24,28},{28,24},{1,5},{5... | collective-permute-start | bytes 1572872 | tf_op jit(solution)/shard_map/ppermute | solution.py:336
